TPU v7x, 128 devices: a whole 4x4x4 slice. The times are simulated.
128 devices in a mesh: dp: 32 (over x, z, core), head: 4 (over y).
Axes of the slice: x: 4, y: 4, z: 4, core: 2. Of those that a mesh axis runs over, the one named last changes fastest.
Arguments:
- layer_input: bfloat16 [96, 1024, 768], P('dp', 'head'), may hold values from -6 to 6
- lengths: int32 [96], P('dp'), may hold values from 64 to 1024, as said below
- cotangent: bfloat16 [96, 1024, 768], P('dp', 'head'), may hold values from -6 to 6
- w_query: bfloat16 [768, 768], replicated, may hold values from -0.21875 to 0.21875
- w_key: bfloat16 [768, 768], replicated, may hold values from -0.21875 to 0.21875
- w_value: bfloat16 [768, 768], replicated, may hold values from -0.21875 to 0.21875
- conv_query: float32 [3, 768], replicated, may hold values from -3 to 3
- conv_key: float32 [3, 768], replicated, may hold values from -3 to 3
- conv_value: float32 [3, 768], replicated, may hold values from -3 to 3
- w_out: bfloat16 [768, 768], replicated, may hold values from -1.75 to 1.75
- w_up: bfloat16 [768, 3072], replicated, may hold values from -0.21875 to 0.21875
- w_down: bfloat16 [3072, 768], replicated, may hold values from -0.109375 to 0.109375
- gain_attn: float32 [768], replicated, may hold values from 0.25 to 1.75
- bias_attn: float32 [768], replicated, may hold values from -1.5 to 1.5
- gain_ffn: float32 [768], replicated, may hold values from 0.25 to 1.75
- bias_ffn: float32 [768], replicated, may hold values from -1.5 to 1.5
Outputs:
- layer_output: bfloat16 [96, 1024, 768], P('dp', 'head')
- input_grad: float32 [96, 1024, 768], P('dp', 'head')
- grad_w_query: float32 [768, 768], replicated
- grad_w_key: float32 [768, 768], replicated
- grad_w_value: float32 [768, 768], replicated
- grad_conv_query: float32 [3, 768], replicated
- grad_conv_key: float32 [3, 768], replicated
- grad_conv_value: float32 [3, 768], replicated
- grad_w_out: float32 [768, 768], replicated
- grad_w_up: float32 [768, 3072], replicated
- grad_w_down: float32 [3072, 768], replicated
- grad_gain_attn: float32 [768], replicated
- grad_bias_attn: float32 [768], replicated
- grad_gain_ffn: float32 [768], replicated
- grad_bias_ffn: float32 [768], replicated
Inputs may be any that keep to these rules, and one draw needn't show every extreme that they name: Of each 3 consecutive sequences (those of one index of dp) one, drawn from the seed, has length exactly 1024; the others follow a law heavily skewed toward short lengths.
All inputs are finite; a program needn't handle non-finite values.
Results may differ from a plain program's by a relative error of at most 0.013.
Values may be sent and summed in bfloat16 or wider, within the bound.
No kernel may reach another device: no remote copies, remote signals or barrier semaphores. Data moves between devices by JAX's collectives and lax.ppermute only.
A program may use at most 256 MiB of HBM per device.

v0:
```python
import jax
import jax.numpy as jnp
from jax import lax
from jax.sharding import PartitionSpec as P

HDIM = 64


def grouped_exchange(array, axis, split_dim, concat_dim, work, item_dim, out_dim):
    items = jax.tree.leaves(array)[0].shape[item_dim]
    count = 2 if items % 2 == 0 else 1
    done = []
    for k in range(count):
        group = jax.tree.map(
            lambda a: lax.slice_in_dim(
                a, k * (items // count), (k + 1) * (items // count), axis=item_dim
            ),
            array,
        )
        done.append(
            work(
                lax.all_to_all(
                    group, axis, split_axis=split_dim, concat_axis=concat_dim, tiled=True
                )
            )
        )
    return jax.tree.map(lambda *parts: jnp.concatenate(parts, axis=out_dim), *done)


def product(left, right):
    return jnp.dot(left, right, preferred_element_type=jnp.float32)


def product_right_t(left, right):
    return lax.dot_general(
        left, right, (((1,), (1,)), ((), ())), preferred_element_type=jnp.float32
    )


def product_left_t(left, right):
    return lax.dot_general(
        left, right, (((0,), (0,)), ((), ())), preferred_element_type=jnp.float32
    )


def norm_forward(rows, gain, bias):
    average = jnp.mean(rows, axis=-1, keepdims=True)
    centred = rows - average
    variance = jnp.mean(centred * centred, axis=-1, keepdims=True)
    inverse = lax.rsqrt(variance + 1e-05)
    unit = centred * inverse
    return (unit * gain + bias, unit, inverse)


def norm_backward(grad_normed, unit, inverse, gain):
    scaled = grad_normed * gain
    mean_grad = jnp.mean(scaled, axis=-1, keepdims=True)
    mean_dot = jnp.mean(scaled * unit, axis=-1, keepdims=True)
    grad_rows = inverse * (scaled - mean_grad - unit * mean_dot)
    return (grad_rows, jnp.sum(grad_normed * unit, axis=0), jnp.sum(grad_normed, axis=0))


def causal_conv(raw, kernel):
    shift_one = jnp.pad(raw, ((1, 0), (0, 0)))[:-1]
    shift_two = jnp.pad(raw, ((2, 0), (0, 0)))[:-2]
    return kernel[0] * raw + kernel[1] * shift_one + kernel[2] * shift_two


def conv_backward(grad, raw, kernel):
    ahead_one = jnp.pad(grad, ((0, 1), (0, 0)))[1:]
    ahead_two = jnp.pad(grad, ((0, 2), (0, 0)))[2:]
    grad_raw = kernel[0] * grad + kernel[1] * ahead_one + kernel[2] * ahead_two
    shift_one = jnp.pad(raw, ((1, 0), (0, 0)))[:-1]
    shift_two = jnp.pad(raw, ((2, 0), (0, 0)))[:-2]
    grad_kernel = jnp.stack(
        [
            jnp.sum(raw * grad, axis=0),
            jnp.sum(shift_one * grad, axis=0),
            jnp.sum(shift_two * grad, axis=0),
        ]
    )
    return (grad_raw.astype(jnp.bfloat16), grad_kernel)


def per_device(
    layer_input,
    lengths,
    cotangent,
    w_query,
    w_key,
    w_value,
    conv_query,
    conv_key,
    conv_value,
    w_out,
    w_up,
    w_down,
    gain_attn,
    bias_attn,
    gain_ffn,
    bias_ffn,
):
    seqs, rows, width = layer_input.shape
    groups = lax.axis_size("head")
    full_len = rows * groups
    columns = width // groups
    heads_here = columns // HDIM
    flat = seqs * rows
    block = min(512, full_len)
    blocks = full_len // block
    score_scale = HDIM ** (-0.5)
    position = lax.axis_index("head") * rows + lax.broadcasted_iota(jnp.int32, (seqs, rows), 1)
    row_mask = (position < lengths[:, None]).astype(jnp.float32).reshape(flat, 1)
    offset = lax.axis_index("head") * columns
    kernels = tuple(
        (
            lax.dynamic_slice_in_dim(kernel, offset, columns, 1)
            for kernel in (conv_query, conv_key, conv_value)
        )
    )

    def causal_mask(start):
        row_ids = start + lax.broadcasted_iota(jnp.int32, (block, full_len), 0)
        col_ids = lax.broadcasted_iota(jnp.int32, (block, full_len), 1)
        return col_ids <= row_ids

    inputs = layer_input.astype(jnp.float32).reshape(flat, width)
    normed, unit_one, inverse_one = norm_forward(inputs, gain_attn, bias_attn)
    normed_low = normed.astype(jnp.bfloat16)
    query_raw = product(normed_low, w_query).astype(jnp.bfloat16).reshape(seqs, rows, width)
    key_raw = product(normed_low, w_key).astype(jnp.bfloat16).reshape(seqs, rows, width)
    value_raw = product(normed_low, w_value).astype(jnp.bfloat16).reshape(seqs, rows, width)

    def attend_one(triple):
        raw_q, raw_k, raw_v = triple
        queries = causal_conv(raw_q.astype(jnp.float32), kernels[0]).astype(jnp.bfloat16)
        keys_all = causal_conv(raw_k.astype(jnp.float32), kernels[1]).astype(jnp.bfloat16)
        values_all = causal_conv(raw_v.astype(jnp.float32), kernels[2]).astype(jnp.bfloat16)
        query_heads = queries.reshape(full_len, heads_here, HDIM)
        key_heads = keys_all.reshape(full_len, heads_here, HDIM)
        value_heads = values_all.reshape(full_len, heads_here, HDIM)

        def forward_block(index):
            start = index * block
            query_block = lax.dynamic_slice_in_dim(query_heads, start, block, 0)
            scores = (
                jnp.einsum(
                    "ihd,jhd->hij", query_block, key_heads, preferred_element_type=jnp.float32
                )
                * score_scale
            )
            scores = jnp.where(causal_mask(start)[None], scores, -1e30)
            top = jnp.max(scores, axis=-1, keepdims=True)
            expo = jnp.exp(scores - top)
            total = jnp.sum(expo, axis=-1, keepdims=True)
            probs = (expo / total).astype(jnp.bfloat16)
            mixed = jnp.einsum(
                "hij,jhd->ihd", probs, value_heads, preferred_element_type=jnp.float32
            )
            return (
                mixed.reshape(block, columns).astype(jnp.bfloat16),
                (top + jnp.log(total))[:, :, 0],
            )

        mixed_blocks, log_totals = lax.map(forward_block, jnp.arange(blocks, dtype=jnp.int32))
        return (mixed_blocks.reshape(full_len, columns), log_totals, queries, keys_all, values_all)

    def attend(pieces):
        mixed, log_totals, queries, keys_all, values_all = lax.map(attend_one, pieces)
        mixed_rows = lax.all_to_all(mixed, "head", split_axis=1, concat_axis=2, tiled=True)
        return (
            mixed_rows,
            log_totals,
            queries,
            keys_all,
            values_all,
            pieces[0],
            pieces[1],
            pieces[2],
        )

    mixed_rows, log_totals, queries, keys_all, values_all, raw_q, raw_k, raw_v = grouped_exchange(
        (query_raw, key_raw, value_raw), "head", 2, 1, attend, 0, 0
    )
    mixed_flat = mixed_rows.reshape(flat, width)
    middle = inputs + product(mixed_flat, w_out)
    normed_two, unit_two, inverse_two = norm_forward(middle, gain_ffn, bias_ffn)
    normed_ffn = normed_two.astype(jnp.bfloat16)
    hidden = product(normed_ffn, w_up)
    squared = jnp.square(jnp.maximum(hidden, 0.0)).astype(jnp.bfloat16)
    result = (middle + product(squared, w_down)) * row_mask
    layer_output = result.astype(jnp.bfloat16).reshape(seqs, rows, width)
    grad_result = cotangent.astype(jnp.float32).reshape(flat, width) * row_mask
    grad_result_low = grad_result.astype(jnp.bfloat16)
    grad_w_down = product_left_t(squared, grad_result_low)
    grad_hidden = (
        product_right_t(grad_result_low, w_down) * 2.0 * jnp.maximum(hidden, 0.0)
    ).astype(jnp.bfloat16)
    grad_w_up = product_left_t(normed_ffn, grad_hidden)
    grad_normed_two = product_right_t(grad_hidden, w_up)
    grad_norm_two, grad_gain_ffn, grad_bias_ffn = norm_backward(
        grad_normed_two, unit_two, inverse_two, gain_ffn
    )
    grad_middle = grad_result + grad_norm_two
    grad_w_up, grad_w_down, grad_gain_ffn, grad_bias_ffn = lax.psum(
        (grad_w_up, grad_w_down, grad_gain_ffn, grad_bias_ffn), ("dp", "head")
    )
    grad_branch = grad_middle.astype(jnp.bfloat16)
    grad_w_out = product_left_t(mixed_flat, grad_branch)
    grad_mixed = product_right_t(grad_branch, w_out).astype(jnp.bfloat16).reshape(seqs, rows, width)
    grad_mixed_heads = lax.all_to_all(grad_mixed, "head", split_axis=2, concat_axis=1, tiled=True)

    def backward_one(bundle):
        grad_att, log_rows, queries_one, keys_one, values_one, raw_qo, raw_ko, raw_vo = bundle
        query_heads = queries_one.reshape(full_len, heads_here, HDIM)
        key_heads = keys_one.reshape(full_len, heads_here, HDIM)
        value_heads = values_one.reshape(full_len, heads_here, HDIM)
        grad_heads = grad_att.reshape(full_len, heads_here, HDIM)

        def backward_block(carry, block_inputs):
            grad_keys, grad_values = carry
            index, log_block = block_inputs
            start = index * block
            query_block = lax.dynamic_slice_in_dim(query_heads, start, block, 0)
            grad_block = lax.dynamic_slice_in_dim(grad_heads, start, block, 0)
            scores = (
                jnp.einsum(
                    "ihd,jhd->hij", query_block, key_heads, preferred_element_type=jnp.float32
                )
                * score_scale
            )
            scores = jnp.where(causal_mask(start)[None], scores, -1e30)
            probs = jnp.exp(scores - log_block[:, :, None])
            grad_probs = jnp.einsum(
                "ihd,jhd->hij", grad_block, value_heads, preferred_element_type=jnp.float32
            )
            row_dot = jnp.sum(probs * grad_probs, axis=-1, keepdims=True)
            grad_scores = (probs * (grad_probs - row_dot)).astype(jnp.bfloat16)
            grad_values = grad_values + jnp.einsum(
                "hij,ihd->jhd",
                probs.astype(jnp.bfloat16),
                grad_block,
                preferred_element_type=jnp.float32,
            )
            grad_keys = (
                grad_keys
                + jnp.einsum(
                    "hij,ihd->jhd", grad_scores, query_block, preferred_element_type=jnp.float32
                )
                * score_scale
            )
            grad_query_block = (
                jnp.einsum(
                    "hij,jhd->ihd", grad_scores, key_heads, preferred_element_type=jnp.float32
                )
                * score_scale
            )
            return ((grad_keys, grad_values), grad_query_block)

        zeros = jnp.zeros((full_len, heads_here, HDIM), jnp.float32)
        (grad_keys, grad_values), grad_query_blocks = lax.scan(
            backward_block, (zeros, zeros), (jnp.arange(blocks, dtype=jnp.int32), log_rows)
        )
        grad_queries = grad_query_blocks.reshape(full_len, columns)
        grad_q_raw, kernel_q = conv_backward(grad_queries, raw_qo.astype(jnp.float32), kernels[0])
        grad_k_raw, kernel_k = conv_backward(
            grad_keys.reshape(full_len, columns), raw_ko.astype(jnp.float32), kernels[1]
        )
        grad_v_raw, kernel_v = conv_backward(
            grad_values.reshape(full_len, columns), raw_vo.astype(jnp.float32), kernels[2]
        )
        return (grad_q_raw, grad_k_raw, grad_v_raw, kernel_q, kernel_k, kernel_v)

    grad_q_heads, grad_k_heads, grad_v_heads, kernel_q, kernel_k, kernel_v = lax.map(
        backward_one,
        (grad_mixed_heads, log_totals, queries, keys_all, values_all, raw_q, raw_k, raw_v),
    )
    kernel_zeros = jnp.zeros((3, width), jnp.float32)
    grad_conv_query = lax.dynamic_update_slice_in_dim(
        kernel_zeros, jnp.sum(kernel_q, axis=0), offset, 1
    )
    grad_conv_key = lax.dynamic_update_slice_in_dim(
        kernel_zeros, jnp.sum(kernel_k, axis=0), offset, 1
    )
    grad_conv_value = lax.dynamic_update_slice_in_dim(
        kernel_zeros, jnp.sum(kernel_v, axis=0), offset, 1
    )
    grad_q_rows, grad_k_rows, grad_v_rows = (
        lax.all_to_all(grad_q_heads, "head", split_axis=1, concat_axis=2, tiled=True),
        lax.all_to_all(grad_k_heads, "head", split_axis=1, concat_axis=2, tiled=True),
        lax.all_to_all(grad_v_heads, "head", split_axis=1, concat_axis=2, tiled=True),
    )
    grad_q_flat = grad_q_rows.reshape(flat, width)
    grad_k_flat = grad_k_rows.reshape(flat, width)
    grad_v_flat = grad_v_rows.reshape(flat, width)
    grad_w_query = product_left_t(normed_low, grad_q_flat)
    grad_w_key = product_left_t(normed_low, grad_k_flat)
    grad_w_value = product_left_t(normed_low, grad_v_flat)
    grad_normed_one = (
        product_right_t(grad_q_flat, w_query)
        + product_right_t(grad_k_flat, w_key)
        + product_right_t(grad_v_flat, w_value)
    )
    grad_norm_one, grad_gain_attn, grad_bias_attn = norm_backward(
        grad_normed_one, unit_one, inverse_one, gain_attn
    )
    input_grad = (grad_middle + grad_norm_one).reshape(seqs, rows, width)
    (
        grad_w_query,
        grad_w_key,
        grad_w_value,
        grad_conv_query,
        grad_conv_key,
        grad_conv_value,
        grad_w_out,
        grad_gain_attn,
        grad_bias_attn,
    ) = lax.psum(
        (
            grad_w_query,
            grad_w_key,
            grad_w_value,
            grad_conv_query,
            grad_conv_key,
            grad_conv_value,
            grad_w_out,
            grad_gain_attn,
            grad_bias_attn,
        ),
        ("dp", "head"),
    )
    return (
        layer_output,
        input_grad,
        grad_w_query,
        grad_w_key,
        grad_w_value,
        grad_conv_query,
        grad_conv_key,
        grad_conv_value,
        grad_w_out,
        grad_w_up,
        grad_w_down,
        grad_gain_attn,
        grad_bias_attn,
        grad_gain_ffn,
        grad_bias_ffn,
    )


def solution(mesh):
    placed = (
        P("dp", "head", None),
        P("dp"),
        P("dp", "head", None),
        P(),
        P(),
        P(),
        P(),
        P(),
        P(),
        P(),
        P(),
        P(),
        P(),
        P(),
        P(),
        P(),
    )
    return jax.shard_map(
        per_device,
        mesh=mesh,
        in_specs=placed,
        out_specs=(
            P("dp", "head", None),
            P("dp", "head", None),
            P(),
            P(),
            P(),
            P(),
            P(),
            P(),
            P(),
            P(),
            P(),
            P(),
            P(),
            P(),
            P(),
        ),
        check_vma=False,
    )
```

profile of v0, /device:TPU:0, one launch (start us, length us, event | category | flops | bytes accessed | tf_op | source)
XLA Modules:
  0.0 895.6 jit_solution(351707590888713220)
XLA Ops:
  27.2 13.4 %all-to-all-done = bf16[3,256,768]{1,0,2:T(4,128)(2,1)S(1)} async-done(((bf16[3,256,768]{1,0,2:T(4,128)(2,1)}), bf16[3,256,768]{1,0,2:T(4,128)(2,1)S(1)}, u32[]{:S(2)}, u32[]{:S(2)}) %all-to-all-start) | async-done | bytes 1179680 | tf_op jit(solution)/shard_map/all_to_all | solution.py:22
  51.9 12.9 %all-to-all-done.1 = bf16[3,256,768]{1,0,2:T(4,128)(2,1)} async-done(((bf16[3,256,768]{1,0,2:T(4,128)(2,1)}), bf16[3,256,768]{1,0,2:T(4,128)(2,1)}, u32[]{:S(2)}, u32[]{:S(2)}) %all-to-all-start.1) | async-done | bytes 1179680 | tf_op jit(solution)/shard_map/all_to_all | solution.py:22
  75.1 13.2 %all-to-all-done.2 = bf16[3,256,768]{1,0,2:T(4,128)(2,1)} async-done(((bf16[3,256,768]{1,0,2:T(4,128)(2,1)}), bf16[3,256,768]{1,0,2:T(4,128)(2,1)}, u32[]{:S(2)}, u32[]{:S(2)}) %all-to-all-start.2) | async-done | bytes 1179680 | tf_op jit(solution)/shard_map/all_to_all | solution.py:22
  94.6 68.3 %while.97 = (s32[]{:T(128)}, bf16[3,1024,192]{2,1,0:T(8,128)(2,1)}, f32[3,2,3,512]{3,2,1,0:T(4,128)}, bf16[3,1024,192]{1,2,0:T(8,128)(2,1)}, bf16[3,1024,192]{1,...) while((s32[]{:T(128)}, bf16[3,1024,192]{2,1,0:T(8,128)(2,1)}, ...), condition=%wide.region_7.8_spmd, body=%wide.region_2.7_spmd.sunk | while | flops 426277888 | bytes 32615152 | solution.py:169
  101.4 14.3 %while.100 = (s32[]{:T(128)}, bf16[2,512,192]{1,2,0:T(8,128)(2,1)S(1)}, f32[2,3,512]{2,1,0:T(4,128)S(1)}, s32[2]{0:T(128)S(1)}, bf16[1024,3,64]{0,2,1:T(8,128)(2...) while((s32[]{:T(128)}, ...), condition=%wide.region_6.6_spmd, body=%wide.region_3.5_spmd.sunk | while | flops 422149120 | bytes 22603968 | solution.py:165
  124.2 14.3 %while.100 = (s32[]{:T(128)}, bf16[2,512,192]{1,2,0:T(8,128)(2,1)S(1)}, f32[2,3,512]{2,1,0:T(4,128)S(1)}, s32[2]{0:T(128)S(1)}, bf16[1024,3,64]{0,2,1:T(8,128)(2...) while((s32[]{:T(128)}, ...), condition=%wide.region_6.6_spmd, body=%wide.region_3.5_spmd.sunk | while | flops 422149120 | bytes 22603968 | solution.py:165
  147.0 14.3 %while.100 = (s32[]{:T(128)}, bf16[2,512,192]{1,2,0:T(8,128)(2,1)S(1)}, f32[2,3,512]{2,1,0:T(4,128)S(1)}, s32[2]{0:T(128)S(1)}, bf16[1024,3,64]{0,2,1:T(8,128)(2...) while((s32[]{:T(128)}, ...), condition=%wide.region_6.6_spmd, body=%wide.region_3.5_spmd.sunk | while | flops 422149120 | bytes 22603968 | solution.py:165
  173.6 20.8 %all-to-all-done.3 = bf16[3,1024,192]{2,0,1:T(4,128)(2,1)S(1)} async-done(((bf16[3,1024,192]{2,0,1:T(4,128)(2,1)}), bf16[3,1024,192]{2,0,1:T(4,128)(2,1)S(1)}, u32[]{:S(2)}, u32[]{:S(2)}) %all-to-all-start.3) | async-done | bytes 1179680 | tf_op jit(solution)/shard_map/all_to_all | solution.py:170
  207.0 9.0 %fusion.109 = f32[768,3072]{1,0:T(8,128)} fusion(bf16[768,3072]{1,0:T(8,128)(2,1)} %param.34, f32[768,768]{1,0:T(8,128)S(1)} %get-tuple-element.759, f32[768]{0:T(1024)S(1)} %copy-done.44, f32[768]{0:T(1024)S(1)} %copy-done.42, f32[768]{0:T(1024)S(1)} %add_rsqrt_fusion, f32[768]{0:T(1024)S(1)} %broadcast_multiply_fusion.4), kind=kOutput, calls=%fused_computation.199 | convolution fusion | flops 3626827776 | bytes 16527360 | tf_op jit(solution)/shard_map/dot_general | solution.py:31
  237.5 17.0 %all-to-all-done.4 = bf16[3,256,768]{1,0,2:T(4,128)(2,1)S(1)} async-done(((bf16[3,256,768]{1,0,2:T(4,128)(2,1)}), bf16[3,256,768]{1,0,2:T(4,128)(2,1)S(1)}, u32[]{:S(2)}, u32[]{:S(2)}) %all-to-all-start.4) | async-done | bytes 1179680 | tf_op jit(solution)/shard_map/all_to_all | solution.py:211
  259.4 257.8 %while.99 = (s32[]{:T(128)}, bf16[3,1024,192]{1,2,0:T(8,128)(2,1)}, bf16[3,1024,192]{1,2,0:T(8,128)(2,1)}, bf16[3,1024,192]{1,2,0:T(8,128)(2,1)}, f32[3,3,192]{2...) while((s32[]{:T(128)}, bf16[3,1024,192]{1,2,0:T(8,128)(2,1)}, ...), condition=%wide.region_25.26_spmd, body=%wide.region_12.25_spmd.sunk | while | flops 1039499968 | bytes 157151312 | solution.py:274
  275.8 51.4 %while.101 = (s32[]{:T(128)}, f32[1024,3,64]{0,2,1:T(8,128)S(1)}, f32[1024,3,64]{0,2,1:T(8,128)}, f32[2,512,3,64]{1,0,3,2:T(2,128)}, s32[2]{0:T(128)S(1)}, /*ind...) while((s32[]{:T(128)}, f32[1024,3,64]{0,2,1:T(8,128)S(1)}, ...), condition=%wide.region_15.15_spmd.clone, body=%wide.region_13.14_spmd.clone.sunk | while | flops 1031830528 | bytes 122470776 | solution.py:261
  293.3 8.1 dynamic_update_slice.126
  319.2 8.1 dynamic_update_slice.126
  358.3 51.4 %while.101 = (s32[]{:T(128)}, f32[1024,3,64]{0,2,1:T(8,128)S(1)}, f32[1024,3,64]{0,2,1:T(8,128)}, f32[2,512,3,64]{1,0,3,2:T(2,128)}, s32[2]{0:T(128)S(1)}, /*ind...) while((s32[]{:T(128)}, f32[1024,3,64]{0,2,1:T(8,128)S(1)}, ...), condition=%wide.region_15.15_spmd.clone, body=%wide.region_13.14_spmd.clone.sunk | while | flops 1031830528 | bytes 122470776 | solution.py:261
  375.7 8.1 dynamic_update_slice.126
  440.7 51.4 %while.101 = (s32[]{:T(128)}, f32[1024,3,64]{0,2,1:T(8,128)S(1)}, f32[1024,3,64]{0,2,1:T(8,128)}, f32[2,512,3,64]{1,0,3,2:T(2,128)}, s32[2]{0:T(128)S(1)}, /*ind...) while((s32[]{:T(128)}, f32[1024,3,64]{0,2,1:T(8,128)S(1)}, ...), condition=%wide.region_15.15_spmd.clone, body=%wide.region_13.14_spmd.clone.sunk | while | flops 1031830528 | bytes 122470776 | solution.py:261
  534.6 12.9 %all-to-all-done.7 = bf16[3,1024,192]{2,0,1:T(4,128)(2,1)} async-done(((bf16[3,1024,192]{2,0,1:T(4,128)(2,1)}), bf16[3,1024,192]{2,0,1:T(4,128)(2,1)}, u32[]{:S(2)}, u32[]{:S(2)}) %all-to-all-start.7) | async-done | bytes 1179680 | tf_op jit(solution)/shard_map/all_to_all | solution.py:291
  551.9 11.6 %fusion.102 = f32[3072,768]{1,0:T(8,128)} fusion(bf16[768,768]{1,0:T(8,128)(2,1)} %fusion.83, f32[768,3072]{1,0:T(8,128)} %fusion.109), kind=kOutput, calls=%fused_computation.179 | convolution fusion | flops 3630956544 | bytes 20054016 | tf_op jit(solution)/shard_map/dot_general | solution.py:41
  576.7 11.0 %fusion.108 = f32[768,3072]{1,0:T(8,128)} fusion(bf16[768,3072]{1,0:T(8,128)(2,1)} %copy-done.19, f32[768,768]{1,0:T(8,128)} %copy-done.12, f32[768]{0:T(1024)S(1)} %copy-done.45, f32[768]{0:T(1024)S(1)} %copy-done.43, f32[768]{0:T(1024)S(1)} %copy-done.41, f32[768]{0:T(1024)S(1)} %copy-done.33), kind=kOutput, calls=%fused_computation.198 | convolution fusion | flops 3626827776 | bytes 16527360 | tf_op jit(solution)/shard_map/dot_general | solution.py:41
  622.4 10.7 %multiply_convert_fusion.3 = bf16[768,768]{1,0:T(8,128)(2,1)} fusion(f32[768,768]{1,0:T(8,128)} %copy-done.12, bf16[3072,768]{1,0:T(8,128)(2,1)} %param.35, f32[768,3072]{1,0:T(8,128)} %fusion.109, f32[768]{0:T(1024)S(1)} %copy-done.58), kind=kOutput, calls=%fused_computation.165 | convolution fusion | flops 3632726016 | bytes 17697792 | tf_op jit(solution)/shard_map/dot_general | solution.py:31
  647.9 68.9 %all-reduce.18 = (f32[3,768]{1,0:T(4,128)}, f32[3,768]{1,0:T(4,128)}, f32[3,768]{1,0:T(4,128)}, f32[768]{0:T(1024)}, f32[768]{0:T(1024)}, /*index=5*/f32[768]{0:T(1024)}, f32[768]{0:T(1024)}) all-reduce(f32[3,768]{1,0:T(4,128)S(1)} %copy-done.49, f32[3,768]{1,0:T(4,128)S(1)} %copy-done.50, ...), channel_id=1, replica_groups=mesh['dp'=32,'head'=4] {'dp','head'}, use_global_device_ids=true, to_apply=%region_32.33 | all-reduce | flops 9984 | bytes 79872 | tf_op jit(solution)/shard_map/psum | solution.py:318
  721.3 144.2 %all-reduce.22.cloned.1.call-done = (f32[768,768]{1,0:T(8,128)}, f32[768,768]{1,0:T(8,128)}, f32[768,768]{1,0:T(8,128)}, f32[768,768]{1,0:T(8,128)}, f32[768,3072]{1,0:T(8,128)}, /*index=5*/f32[3072,768]{1,0:T(8,128)}) async-done(((f32[768,768]{1,0:T(8,128)}, f32[768,768]{1,0:T(8,128)}, f32[768,768]{1,0:T(8,128)}, f32[768,768]{1,0:T(8,128)}, f32[768,3072]{1,0:T(8,128)}, /*index=5*/f32[3072,768]{1,0:T(8,128)}), ...) | async-done | bytes 28311568 | tf_op jit(solution)/shard_map/psum | solution.py:318
  875.4 9.3 %copy.232 = f32[768,3072]{1,0:T(8,128)} copy(f32[768,3072]{1,0:T(8,128)} %get-tuple-element.1392) | data formatting | bytes 18874368
  (556 shorter events, 481.7 us)
Async XLA Ops:
  7.2 37.8 %copy-start = (bf16[768,768]{1,0:T(8,128)(2,1)S(1)}, bf16[768,768]{1,0:T(8,128)(2,1)}, u32[]{:S(2)}) copy-start(bf16[768,768]{1,0:T(8,128)(2,1)} %param.29) | copy-start | bytes 3538948
  15.3 25.3 %all-to-all-start = ((bf16[3,256,768]{1,0,2:T(4,128)(2,1)}), bf16[3,256,768]{1,0,2:T(4,128)(2,1)S(1)}, u32[]{:S(2)}, u32[]{:S(2)}) async-start(bf16[3,256,768]{1,0,2:T(4,128)(2,1)} %copy.75), calls=%async_computation | async-start | bytes 3145728 | tf_op jit(solution)/shard_map/all_to_all | solution.py:22
  40.6 24.2 %all-to-all-start.1 = ((bf16[3,256,768]{1,0,2:T(4,128)(2,1)}), bf16[3,256,768]{1,0,2:T(4,128)(2,1)}, u32[]{:S(2)}, u32[]{:S(2)}) async-start(bf16[3,256,768]{1,0,2:T(4,128)(2,1)} %copy.78), calls=%async_computation.1 | async-start | bytes 3145728 | tf_op jit(solution)/shard_map/all_to_all | solution.py:22
  64.8 23.5 %all-to-all-start.2 = ((bf16[3,256,768]{1,0,2:T(4,128)(2,1)}), bf16[3,256,768]{1,0,2:T(4,128)(2,1)}, u32[]{:S(2)}, u32[]{:S(2)}) async-start(bf16[3,256,768]{1,0,2:T(4,128)(2,1)} %copy.81), calls=%async_computation.2 | async-start | bytes 3145728 | tf_op jit(solution)/shard_map/all_to_all | solution.py:22
  167.0 27.5 %all-to-all-start.3 = ((bf16[3,1024,192]{2,0,1:T(4,128)(2,1)}), bf16[3,1024,192]{2,0,1:T(4,128)(2,1)S(1)}, u32[]{:S(2)}, u32[]{:S(2)}) async-start(bf16[3,1024,192]{2,0,1:T(4,128)(2,1)} %copy.85), calls=%async_computation.3 | async-start | bytes 4194304 | tf_op jit(solution)/shard_map/all_to_all | solution.py:170
  171.0 58.0 %copy-start.57 = (f32[768]{0:T(1024)}, f32[768]{0:T(1024)S(1)}, u32[]{:S(2)}) copy-start(f32[768]{0:T(1024)S(1)} %reshape.405) | copy-start | bytes 9220
  206.2 22.9 %copy-start.12 = (f32[768,768]{1,0:T(8,128)}, f32[768,768]{1,0:T(8,128)S(1)}, u32[]{:S(2)}) copy-start(f32[768,768]{1,0:T(8,128)S(1)} %get-tuple-element.759) | copy-start | bytes 7077892
  206.2 22.8 %copy-start.32 = (f32[768]{0:T(1024)}, f32[768]{0:T(1024)S(1)}, u32[]{:S(2)}) copy-start(f32[768]{0:T(1024)S(1)} %broadcast_multiply_fusion.4) | copy-start | bytes 9220
  207.0 22.1 %copy-start.40 = (f32[768]{0:T(1024)}, f32[768]{0:T(1024)S(1)}, u32[]{:S(2)}) copy-start(f32[768]{0:T(1024)S(1)} %add_rsqrt_fusion) | copy-start | bytes 9220
  207.0 17.0 %slice-start.3 = ((s8[4718592]{0:T(1024)(128)(4,1)}), s8[4194304]{0:T(1024)(128)(4,1)S(1)}, s32[]{:S(2)}) async-start(s8[4718592]{0:T(1024)(128)(4,1)} %bitcast.412), calls=%async_computation.12 | async-start | bytes 8388608
  233.9 20.6 %all-to-all-start.4 = ((bf16[3,256,768]{1,0,2:T(4,128)(2,1)}), bf16[3,256,768]{1,0,2:T(4,128)(2,1)S(1)}, u32[]{:S(2)}, u32[]{:S(2)}) async-start(bf16[3,256,768]{1,0,2:T(4,128)(2,1)} %copy.87), calls=%async_computation.4 | async-start | bytes 3145728 | tf_op jit(solution)/shard_map/all_to_all | solution.py:211
  521.3 26.1 %all-to-all-start.7 = ((bf16[3,1024,192]{2,0,1:T(4,128)(2,1)}), bf16[3,1024,192]{2,0,1:T(4,128)(2,1)}, u32[]{:S(2)}, u32[]{:S(2)}) async-start(bf16[3,1024,192]{2,0,1:T(4,128)(2,1)} %copy.94), calls=%async_computation.7 | async-start | bytes 4194304 | tf_op jit(solution)/shard_map/all_to_all | solution.py:291
  547.4 24.7 %all-to-all-start.5 = ((bf16[3,1024,192]{2,0,1:T(4,128)(2,1)}), bf16[3,1024,192]{2,0,1:T(4,128)(2,1)}, u32[]{:S(2)}, u32[]{:S(2)}) async-start(bf16[3,1024,192]{2,0,1:T(4,128)(2,1)} %copy.90), calls=%async_computation.5 | async-start | bytes 4194304 | tf_op jit(solution)/shard_map/all_to_all | solution.py:289
  551.9 11.6 %copy-start.18 = (bf16[3,1024,192]{1,2,0:T(8,128)(2,1)S(1)}, bf16[3,1024,192]{1,2,0:T(8,128)(2,1)}, u32[]{:S(2)}) copy-start(bf16[3,1024,192]{1,2,0:T(8,128)(2,1)} %get-tuple-element.492) | copy-start | bytes 3538948
  566.0 10.7 %copy-start.33 = (f32[768]{0:T(1024)S(1)}, f32[768]{0:T(1024)}, u32[]{:S(2)}) copy-start(f32[768]{0:T(1024)} %copy-done.32) | copy-start | bytes 9220
  566.0 10.7 %copy-start.41 = (f32[768]{0:T(1024)S(1)}, f32[768]{0:T(1024)}, u32[]{:S(2)}) copy-start(f32[768]{0:T(1024)} %copy-done.40) | copy-start | bytes 9220
  566.0 10.7 %copy-start.43 = (f32[768]{0:T(1024)S(1)}, f32[768]{0:T(1024)}, u32[]{:S(2)}) copy-start(f32[768]{0:T(1024)} %param.38) | copy-start | bytes 9220
  566.0 10.7 %copy-start.45 = (f32[768]{0:T(1024)S(1)}, f32[768]{0:T(1024)}, u32[]{:S(2)}) copy-start(f32[768]{0:T(1024)} %param.39) | copy-start | bytes 9220
  572.2 32.0 %all-to-all-start.6 = ((bf16[3,1024,192]{2,0,1:T(4,128)(2,1)}), bf16[3,1024,192]{2,0,1:T(4,128)(2,1)}, u32[]{:S(2)}, u32[]{:S(2)}) async-start(bf16[3,1024,192]{2,0,1:T(4,128)(2,1)} %copy.92), calls=%async_computation.6 | async-start | bytes 4194304 | tf_op jit(solution)/shard_map/all_to_all | solution.py:290
  576.6 288.9 %all-reduce.22.cloned.1.call-start = ((), (), s32[]{:S(2)}) async-start(), calls=%async_computation.8 | async-start | bytes 56623104 | tf_op jit(solution)/shard_map/psum | solution.py:318
  622.4 18.3 %copy-start.29 = (bf16[768,768]{1,0:T(8,128)(2,1)S(1)}, bf16[768,768]{1,0:T(8,128)(2,1)}, u32[]{:S(2)}) copy-start(bf16[768,768]{1,0:T(8,128)(2,1)} %reshape.392) | copy-start | bytes 3538948
  874.0 10.7 %slice-start = ((s8[9437184]{0:T(1024)(128)(4,1)}), s8[4194304]{0:T(1024)(128)(4,1)S(1)}, s32[]{:S(2)}) async-start(s8[9437184]{0:T(1024)(128)(4,1)} %bitcast.368), calls=%async_computation.9 | async-start | bytes 8388608
  875.4 9.3 %slice-start.1 = ((s8[9437184]{0:T(1024)(128)(4,1)}), s8[4194304]{0:T(1024)(128)(4,1)S(1)}, s32[]{:S(2)}) async-start(s8[9437184]{0:T(1024)(128)(4,1)} %bitcast.368), calls=%async_computation.10 | async-start | bytes 8388608
  875.4 9.3 %slice-start.2 = ((s8[9437184]{0:T(1024)(128)(4,1)}), s8[1048576]{0:T(1024)(128)(4,1)S(1)}, s32[]{:S(2)}) async-start(s8[9437184]{0:T(1024)(128)(4,1)} %bitcast.368), calls=%async_computation.11 | async-start | bytes 2097152
  (90 other events, 303.3 us)
Sparse Core Ops, SparseCore 0:
  621.8 243.7 all-reduce.21
where the time goes:
time: 903 us; the launch traced here: 896 us
  waiting for transfers between devices  241 us (27%)
  local copies, waits for them, and re-layouts  206 us (23%)
  matrix products  179 us (20%)
  other arithmetic  133 us (15%)
  blocking collectives  68.9 us (8%)
  starting transfers between devices  34.5 us (4%)
  loops' own time  19.5 us (2%)
  between operations  15.1 us (2%)
    psum x1, waiting for transfers between devices, per_device(): lax.psum((grad_w_query, grad_w_key, grad_w_value, grad_conv_query, grad_c...  144 us
    psum x1, blocking collectives, per_device(): lax.psum((grad_w_query, grad_w_key, grad_w_value, grad_conv_query, grad_c...  68.9 us
    dynamic_update_slice x12, local copies, waits for them, and re-layouts, backward_one(): lax.scan(backward_block, (zeros, zeros), (jnp.arange(blocks, dtype=jnp.in...  50.9 us
    all_to_all x3, waiting for transfers between devices, grouped_exchange(): lax.all_to_all(group, axis, split_axis=split_dim, concat_axis=concat_dim,...  39.6 us
    dot_general x6, matrix products, product_left_t(): lax.dot_general(left, right, (((0,), (0,)), ((), ())), preferred_element_...  35.5 us
    dot_general x6, matrix products, product(): return jnp.dot(left, right, preferred_element_type=jnp.float32)  30.8 us
    unnamed x138, local copies, waits for them, and re-layouts  27.3 us
    dot_general x6, matrix products, backward_block(): jnp.einsum('hij,ihd->jhd', probs.astype(jnp.bfloat16), grad_block, prefer...  25 us
  transfers between devices with their start and end apart: 9, of which 8 were waited for; matrix products, arithmetic and copies ran while one was open for 11% of the time, Pallas kernels for 0%

commit v1 on v0

v1 whole, which is shorter than its diff:
```python
import functools

import jax
import jax.numpy as jnp
from jax import lax
from jax.experimental import pallas as pl
from jax.experimental.pallas import tpu as pltpu
from jax.sharding import Mesh
from jax.sharding import PartitionSpec as P

HDIM = 64
GROUPS = 4
BLOCK = 256
FULL = 1024
WIDTH = 768
COLS = 192
FF = 3072
SEQS = 3
CHUNK = 512
HEADS_HERE = 3
PACK_ROWS = 640
F32 = jnp.float32
BF16 = jnp.bfloat16
NN = (((1,), (0,)), ((), ()))
NT = (((1,), (1,)), ((), ()))
TN = (((0,), (0,)), ((), ()))


def dot(left, right, dims):
    return lax.dot_general(left, right, dims, preferred_element_type=F32)


def cost(flops, nbytes, transcendentals=0):
    return pl.CostEstimate(
        flops=int(flops), bytes_accessed=int(nbytes), transcendentals=int(transcendentals)
    )


def vmem():
    return pl.BlockSpec(memory_space=pltpu.VMEM)


def params(mib):
    return pltpu.CompilerParams(vmem_limit_bytes=mib << 20)


def unit_rows(rows):
    average = jnp.mean(rows, axis=-1, keepdims=True)
    centred = rows - average
    variance = jnp.mean(centred * centred, axis=-1, keepdims=True)
    inverse = lax.rsqrt(variance + 1e-05)
    return centred * inverse, inverse


def head_masks():
    lane = lax.broadcasted_iota(jnp.int32, (1, COLS), 1)
    return [
        jnp.where((lane >= h * HDIM) & (lane < (h + 1) * HDIM), 1.0, 0.0).astype(F32)
        for h in range(HEADS_HERE)
    ]


def conv_rows(raw_f, taps, tap_row, start):
    total = taps[tap_row : tap_row + 1, :] * raw_f[8 + start : 8 + start + BLOCK, :]
    for m in (1, 2):
        total += (
            taps[tap_row + m : tap_row + m + 1, :]
            * raw_f[8 + start - m : 8 + start - m + BLOCK, :]
        )
    return total


def attend_kernel(
    info, x0, x1, x2_lo, x2_hi, x3, w_mine, taps, gain, bias,
    normed, raw_q, raw_k, raw_v, mixed, m0, m_next, m_prev, lse_t,
    pad_q, pad_k, pad_v, q_s, k_s, v_s, below,
):
    here, length = info[0], info[1]
    blocks = (length + BLOCK - 1) // BLOCK
    masks = head_masks()

    for piece, ahead, shift in ((x0, 0, 0), (x1, 1, 0), (x2_lo, 2, 0), (x2_hi, 2, 128), (x3, 3, 0)):
        home = lax.rem(here + ahead, GROUPS)
        size = piece.shape[-2]

        @pl.when(home < blocks)
        def _(piece=piece, home=home, shift=shift, size=size):
            rows = piece[...].reshape(size, WIDTH).astype(F32)
            unit, _ = unit_rows(rows)
            low = (unit * gain[...] + bias[...]).astype(BF16)
            at = pl.multiple_of(home * BLOCK + shift, 128)
            normed[pl.ds(at, size), :] = low
            for n, (raw, pad) in enumerate(((raw_q, pad_q), (raw_k, pad_k), (raw_v, pad_v))):
                value = dot(low, w_mine[n * COLS : (n + 1) * COLS, :], NT).astype(BF16)
                raw[pl.ds(at, size), :] = value
                pad[pl.ds(at + 8, size), :] = value.astype(F32)

    for pad in (pad_q, pad_k, pad_v):
        pad[0:8, :] = jnp.zeros((8, COLS), F32)
    row = lax.broadcasted_iota(jnp.int32, (BLOCK, BLOCK), 0)
    col = lax.broadcasted_iota(jnp.int32, (BLOCK, BLOCK), 1)
    below[...] = jnp.where(col <= row, 0.0, -1e30).astype(F32)

    for b in range(GROUPS):

        @pl.when(b < blocks)
        def _(b=b):
            at = slice(b * BLOCK, (b + 1) * BLOCK)
            q_s[at, :] = (conv_rows(pad_q, taps, 0, b * BLOCK).astype(BF16).astype(F32) * 0.125).astype(BF16)
            k_s[at, :] = conv_rows(pad_k, taps, 3, b * BLOCK).astype(BF16)
            v_s[at, :] = conv_rows(pad_v, taps, 6, b * BLOCK).astype(BF16)
            reach = (b + 1) * BLOCK
            lane = lax.broadcasted_iota(jnp.int32, (BLOCK, 128), 1)
            total_out = jnp.zeros((BLOCK, COLS), F32)
            logs = jnp.zeros((BLOCK, 128), F32)
            for h in range(HEADS_HERE):
                q_h = q_s[at, :] * masks[h].astype(BF16)
                diag = dot(q_h, k_s[at, :], NT) + below[...]
                top = jnp.max(diag, axis=-1, keepdims=True)
                if b:
                    left = dot(q_h, k_s[0 : b * BLOCK, :], NT)
                    top = jnp.maximum(top, jnp.max(left, axis=-1, keepdims=True))
                    expo_left = jnp.exp(left - top)
                expo = jnp.exp(diag - top)
                total = jnp.sum(expo, axis=-1, keepdims=True)
                out = dot(expo.astype(BF16), v_s[at, :], NN)
                if b:
                    total += jnp.sum(expo_left, axis=-1, keepdims=True)
                    out += dot(expo_left.astype(BF16), v_s[0 : b * BLOCK, :], NN)
                total_out = total_out + (out * masks[h]) * (1.0 / total)
                logs = jnp.where(lane == h, top + jnp.log(total), logs)
            mixed[at, :] = total_out.astype(BF16)
            lse_t[:, at] = jnp.transpose(logs)[0:8, :]

        @pl.when(b >= blocks)
        def _(b=b):
            mixed[b * BLOCK : (b + 1) * BLOCK, :] = jnp.zeros((BLOCK, COLS), BF16)

    def rows_of(ahead, shift, size):
        at = pl.multiple_of(lax.rem(here + ahead, GROUPS) * BLOCK + shift, 128)
        return mixed[pl.ds(at, size), :]

    m0[...] = rows_of(0, 0, BLOCK)
    m_next[0:BLOCK, :] = rows_of(1, 0, BLOCK)
    m_next[BLOCK:, :] = rows_of(2, 0, 128)
    m_prev[0:BLOCK, :] = rows_of(3, 0, BLOCK)
    m_prev[BLOCK:, :] = rows_of(2, 128, 128)


def attend(info, pieces, w_mine, taps, gain, bias):
    low = lambda *shape: jax.ShapeDtypeStruct(shape, BF16)
    return pl.pallas_call(
        attend_kernel,
        out_shape=(
            low(FULL, WIDTH),
            low(FULL, COLS), low(FULL, COLS), low(FULL, COLS),
            low(FULL, COLS),
            low(BLOCK, COLS), low(BLOCK + 128, COLS), low(BLOCK + 128, COLS),
            jax.ShapeDtypeStruct((8, FULL), F32),
        ),
        in_specs=[pl.BlockSpec(memory_space=pltpu.SMEM)] + [vmem()] * 9,
        out_specs=[vmem()] * 9,
        scratch_shapes=[pltpu.VMEM((FULL + 8, COLS), F32)] * 3
        + [pltpu.VMEM((FULL, COLS), BF16)] * 3
        + [pltpu.VMEM((BLOCK, BLOCK), F32)],
        compiler_params=params(40),
        cost_estimate=cost(3e9, 8e6, 2e6),
        name="attend",
    )(info, *pieces, w_mine, taps, gain, bias)


def attend_back_kernel(
    first, last,
    info, g0, g_next, g_over, g_prev, g_under, normed, raw_q, raw_k, raw_v, mixed, lse_t,
    w_mine, taps, gain, bias, ffn_vectors, dw_in, small_in,
    d0, d_next, d_prev, dw_out, small_out, *scratch,
):
    if last:
        pack_out, scratch = scratch[0], scratch[1:]
    pad_q, pad_k, pad_v, q_s, k_s, v_s, g_s, dq_s, dk_s, dv_s, d_all, below = scratch
    here, length = info[0], info[1]
    blocks = (length + BLOCK - 1) // BLOCK
    masks = head_masks()

    for piece, start, ahead, shift, size in (
        (g0, 0, 0, 0, BLOCK),
        (g_next, 0, 3, 0, BLOCK),
        (g_over, 0, 2, 0, 128),
        (g_prev, 0, 1, 0, BLOCK),
        (g_under, 0, 2, 128, 128),
    ):
        at = pl.multiple_of(lax.rem(here + ahead, GROUPS) * BLOCK + shift, 128)
        g_s[pl.ds(at, size), :] = piece[start : start + size, :]

    row = lax.broadcasted_iota(jnp.int32, (BLOCK, BLOCK), 0)
    col = lax.broadcasted_iota(jnp.int32, (BLOCK, BLOCK), 1)
    below[...] = jnp.where(row <= col, 0.0, -1e30).astype(F32)
    for pad, raw in ((pad_q, raw_q), (pad_k, raw_k), (pad_v, raw_v)):
        pad[0:8, :] = jnp.zeros((8, COLS), F32)
    for total in (dq_s, dk_s, dv_s):
        total[...] = jnp.zeros((FULL + 8, COLS), F32)

    for b in range(GROUPS):

        @pl.when(b < blocks)
        def _(b=b):
            at = slice(b * BLOCK, (b + 1) * BLOCK)
            for pad, raw in ((pad_q, raw_q), (pad_k, raw_k), (pad_v, raw_v)):
                pad[8 + b * BLOCK : 8 + (b + 1) * BLOCK, :] = raw[at, :].astype(F32)
            q_s[at, :] = (conv_rows(pad_q, taps, 0, b * BLOCK).astype(BF16).astype(F32) * 0.125).astype(BF16)
            k_s[at, :] = conv_rows(pad_k, taps, 3, b * BLOCK).astype(BF16)
            v_s[at, :] = conv_rows(pad_v, taps, 6, b * BLOCK).astype(BF16)
            g_here = g_s[at, :]
            both = jnp.transpose(g_here.astype(F32) * mixed[at, :].astype(F32))
            dq_total = jnp.zeros((BLOCK, COLS), F32)
            for h in range(HEADS_HERE):
                mask_low = masks[h].astype(BF16)
                q_h = q_s[at, :] * mask_low
                g_h = g_here * mask_low
                row_dot = jnp.sum(both[h * HDIM : (h + 1) * HDIM, :], axis=0, keepdims=True)
                log_row = lse_t[h : h + 1, at]
                dq_h = jnp.zeros((BLOCK, COLS), F32)
                for j in range(b + 1):
                    keys = slice(j * BLOCK, (j + 1) * BLOCK)
                    scores = dot(k_s[keys, :], q_h, NT)
                    if j == b:
                        scores = scores + below[...]
                    probs = jnp.exp(scores - log_row)
                    grad_probs = dot(v_s[keys, :], g_h, NT)
                    grad_scores = (probs * (grad_probs - row_dot)).astype(BF16)
                    dv_s[keys, :] += dot(probs.astype(BF16), g_h, NN)
                    dk_s[keys, :] += dot(grad_scores, q_h, NN)
                    dq_h += dot(grad_scores, k_s[keys, :], TN)
                dq_total += dq_h * masks[h]
            dq_s[at, :] = dq_total * 0.125

    if first:
        dw_out[...] = jnp.zeros_like(dw_out)
        small_out[...] = jnp.zeros_like(small_out)
    else:
        dw_out[...] = dw_in[...]
        small_out[...] = small_in[...]

    for b in range(GROUPS):

        @pl.when(b < blocks)
        def _(b=b):
            start = b * BLOCK
            at = slice(start, start + BLOCK)
            parts = []
            for n, (pad, grad) in enumerate(((pad_q, dq_s), (pad_k, dk_s), (pad_v, dv_s))):
                now = grad[at, :]
                value = taps[3 * n : 3 * n + 1, :] * now
                for m in (1, 2):
                    value += taps[3 * n + m : 3 * n + m + 1, :] * grad[start + m : start + m + BLOCK, :]
                parts.append(value.astype(BF16))
                for m in range(3):
                    shifted = pad[8 + start - m : 8 + start - m + BLOCK, :]
                    small_out[3 * n + m : 3 * n + m + 1, 0:COLS] += jnp.sum(
                        shifted * now, axis=0, keepdims=True
                    )
            joined = jnp.concatenate(parts, axis=1)
            d_all[at, :] = joined
            small_out[9:10, 0 : 3 * COLS] += jnp.sum(joined.astype(F32), axis=0, keepdims=True)
            dw_out[...] += dot(joined, normed[at, :], TN)

        @pl.when(b >= blocks)
        def _(b=b):
            d_all[b * BLOCK : (b + 1) * BLOCK, :] = jnp.zeros((BLOCK, 3 * COLS), BF16)

    def rows_of(ahead, shift, size):
        at = pl.multiple_of(lax.rem(here + ahead, GROUPS) * BLOCK + shift, 128)
        return d_all[pl.ds(at, size), :]

    d0[...] = rows_of(0, 0, BLOCK)
    d_next[0:BLOCK, :] = rows_of(1, 0, BLOCK)
    d_next[BLOCK:, :] = rows_of(2, 0, 128)
    d_prev[0:BLOCK, :] = rows_of(3, 0, BLOCK)
    d_prev[BLOCK:, :] = rows_of(2, 128, 128)

    if last:
        sums = small_out[9:10, 0 : 3 * COLS]
        high = sums.astype(BF16)
        rest = (sums - high.astype(F32)).astype(BF16)
        grad_bias = dot(jnp.broadcast_to(high, (8, 3 * COLS)), w_mine[...], NN)[0:1, :]
        grad_bias += dot(jnp.broadcast_to(rest, (8, 3 * COLS)), w_mine[...], NN)[0:1, :]
        grad_normed = jnp.sum(w_mine[...].astype(F32) * dw_out[...], axis=0, keepdims=True)
        grad_gain = (grad_normed - bias[...] * grad_bias) / gain[...]
        pack_out[0 : 3 * COLS, :] = dw_out[...].astype(BF16)
        tail = jnp.concatenate(
            [
                small_out[0:9, :],
                grad_gain,
                grad_bias,
                ffn_vectors[0:2, :],
                jnp.zeros((3, WIDTH), F32),
            ],
            axis=0,
        )
        pack_out[3 * COLS : 3 * COLS + 16, :] = tail.astype(BF16)
        pack_out[3 * COLS + 16 :, :] = jnp.zeros((PACK_ROWS - 3 * COLS - 16, WIDTH), BF16)


def attend_back(first, last, info, grads, saved, w_mine, taps, gain, bias, ffn_vectors, dw, small):
    low = lambda *shape: jax.ShapeDtypeStruct(shape, BF16)
    full = lambda *shape: jax.ShapeDtypeStruct(shape, F32)
    out_shape = [
        low(BLOCK, 3 * COLS), low(BLOCK + 128, 3 * COLS), low(BLOCK + 128, 3 * COLS),
        full(3 * COLS, WIDTH), full(16, WIDTH),
    ]
    if last:
        out_shape.append(low(PACK_ROWS, WIDTH))
    return pl.pallas_call(
        functools.partial(attend_back_kernel, first, last),
        out_shape=out_shape,
        in_specs=[pl.BlockSpec(memory_space=pltpu.SMEM)] + [vmem()] * 18,
        out_specs=[vmem()] * len(out_shape),
        scratch_shapes=[pltpu.VMEM((FULL + 8, COLS), F32)] * 3
        + [pltpu.VMEM((FULL, COLS), BF16)] * 4
        + [pltpu.VMEM((FULL + 8, COLS), F32)] * 3
        + [pltpu.VMEM((FULL, 3 * COLS), BF16)]
        + [pltpu.VMEM((BLOCK, BLOCK), F32)],
        compiler_params=params(48),
        cost_estimate=cost(5e9, 1.2e7, 2e6),
        name="attend_back",
    )(info, *grads, *saved, w_mine, taps, gain, bias, ffn_vectors, dw, small)


def ffn_kernel(
    info, x, cotangent, *refs,
):
    pieces, refs = refs[: 5 * SEQS], refs[5 * SEQS :]
    (
        w_out, gain, bias, w_up, w_down,
        layer_output, grad_middle, g0, g_next, g_prev,
        send, keep, send_out, keep_out, vectors,
        middle, normed, low_grad, total_out, total_grad, sq_s, gh_s, branch, dw_out, mixed_s,
    ) = refs
    step = pl.program_id(0)
    here, core = info[0], info[1]

    def w_out_rows(ahead):
        at = pl.multiple_of(lax.rem(here + ahead, GROUPS) * COLS, 64)
        return pl.ds(at, COLS)

    @pl.when(step == 0)
    def _():
        for s in range(SEQS):
            at = slice(s * BLOCK, (s + 1) * BLOCK)
            m0, m_next, m_over, m_prev, m_under = pieces[5 * s : 5 * s + 5]
            mixed_s[0, at, :] = m0[...]
            mixed_s[3, at, :] = m_next[0:BLOCK, :]
            mixed_s[2, s * BLOCK : s * BLOCK + 128, :] = m_over[...]
            mixed_s[2, s * BLOCK + 128 : (s + 1) * BLOCK, :] = m_under[...]
            mixed_s[1, at, :] = m_prev[0:BLOCK, :]
            value = x[s].astype(F32)
            for k in range(GROUPS):
                value += dot(mixed_s[k, at, :], w_out[w_out_rows(k), :], NN)
            middle[at, :] = value
            unit, _ = unit_rows(value)
            normed[at, :] = (unit * gain[...] + bias[...]).astype(BF16)
            position = here * BLOCK + lax.broadcasted_iota(jnp.int32, (BLOCK, 1), 0)
            keep_row = position < info[2 + s]
            low_grad[at, :] = jnp.where(keep_row, cotangent[s].astype(F32), 0.0).astype(BF16)
            total_out[at, :] = jnp.zeros((BLOCK, WIDTH), F32)
            total_grad[at, :] = jnp.zeros((BLOCK, WIDTH), F32)

    for s in range(SEQS):
        at = slice(s * BLOCK, (s + 1) * BLOCK)
        hidden = jnp.maximum(dot(normed[at, :], w_up[...], NN), 0.0)
        squared = (hidden * hidden).astype(BF16)
        sq_s[at, :] = squared
        total_out[at, :] += dot(squared, w_down[...], NN)
        back = dot(low_grad[at, :], w_down[...], NT)
        grad_hidden = (back * 2.0 * hidden).astype(BF16)
        gh_s[at, :] = grad_hidden
        total_grad[at, :] += dot(grad_hidden, w_up[...], NT)
    grad_up = dot(gh_s[...], normed[...], TN).astype(BF16)
    grad_down = dot(sq_s[...], low_grad[...], TN).astype(BF16)

    @pl.when(step < 3)
    def _():
        send[0] = grad_up
        send[1] = grad_down

    @pl.when(step >= 3)
    def _():
        keep[0] = grad_up
        keep[1] = grad_down

    @pl.when(step == 5)
    def _():
        sum_gain = jnp.zeros((1, WIDTH), F32)
        sum_bias = jnp.zeros((1, WIDTH), F32)
        for s in range(SEQS):
            at = slice(s * BLOCK, (s + 1) * BLOCK)
            position = here * BLOCK + lax.broadcasted_iota(jnp.int32, (BLOCK, 1), 0)
            keep_row = position < info[2 + s]
            layer_output[s] = jnp.where(keep_row, middle[at, :] + total_out[at, :], 0.0).astype(BF16)
            unit, inverse = unit_rows(middle[at, :])
            grad_normed = total_grad[at, :]
            scaled = grad_normed * gain[...]
            mean_grad = jnp.mean(scaled, axis=-1, keepdims=True)
            mean_dot = jnp.mean(scaled * unit, axis=-1, keepdims=True)
            value = low_grad[at, :].astype(F32) + inverse * (scaled - mean_grad - unit * mean_dot)
            sum_gain += jnp.sum(grad_normed * unit, axis=0, keepdims=True)
            sum_bias += jnp.sum(grad_normed, axis=0, keepdims=True)
            grad_middle[s] = value
            branch[at, :] = value.astype(BF16)
            low = branch[at, :]
            g0[s] = dot(low, w_out[w_out_rows(0), :], NT).astype(BF16)
            g_next[s, 0:BLOCK, :] = dot(low, w_out[w_out_rows(1), :], NT).astype(BF16)
            over = dot(low, w_out[w_out_rows(2), :], NT).astype(BF16)
            g_next[s, BLOCK:, :] = over[0:128]
            g_prev[s, BLOCK:, :] = over[128:]
            g_prev[s, 0:BLOCK, :] = dot(low, w_out[w_out_rows(3), :], NT).astype(BF16)
        vectors[...] = jnp.concatenate(
            [sum_gain, sum_bias, jnp.zeros((6, WIDTH), F32)], axis=0
        )
        for k in range(GROUPS):
            dw_out[w_out_rows(k), :] = dot(mixed_s[k], branch[...], TN).astype(BF16)
        half = WIDTH // 2
        keep_out[...] = dw_out[pl.ds(pl.multiple_of(core * half, 128), half), :]
        send_out[...] = dw_out[pl.ds(pl.multiple_of((1 - core) * half, 128), half), :]


def ffn(info, x, cotangent, pieces, w_out, gain, bias, w_up, w_down):
    low = lambda *shape: jax.ShapeDtypeStruct(shape, BF16)
    full = lambda *shape: jax.ShapeDtypeStruct(shape, F32)
    rows = SEQS * BLOCK
    steps = FF // CHUNK
    half = steps // 2

    def chunk(i, sc):
        side = jnp.where(i < half, 1 - sc[1], sc[1])
        return side * half + lax.rem(i, half)

    whole = lambda shape: pl.BlockSpec(shape, lambda i, sc: (0,) * len(shape))
    piece_shapes = [p.shape for p in pieces]
    grid_spec = pltpu.PrefetchScalarGridSpec(
        num_scalar_prefetch=1,
        grid=(steps,),
        in_specs=[whole((SEQS, BLOCK, WIDTH)), whole((SEQS, BLOCK, WIDTH))]
        + [whole(s) for s in piece_shapes]
        + [
            whole((WIDTH, WIDTH)), whole((1, WIDTH)), whole((1, WIDTH)),
            pl.BlockSpec((WIDTH, CHUNK), lambda i, sc: (0, chunk(i, sc))),
            pl.BlockSpec((CHUNK, WIDTH), lambda i, sc: (chunk(i, sc), 0)),
        ],
        out_specs=[
            whole((SEQS, BLOCK, WIDTH)), whole((SEQS, BLOCK, WIDTH)),
            whole((SEQS, BLOCK, COLS)), whole((SEQS, BLOCK + 128, COLS)), whole((SEQS, BLOCK + 128, COLS)),
            pl.BlockSpec((2, CHUNK, WIDTH), lambda i, sc: (0, jnp.minimum(i, half - 1), 0)),
            pl.BlockSpec((2, CHUNK, WIDTH), lambda i, sc: (0, jnp.maximum(i - half, 0), 0)),
            whole((WIDTH // 2, WIDTH)), whole((WIDTH // 2, WIDTH)),
            whole((8, WIDTH)),
        ],
        scratch_shapes=[
            pltpu.VMEM((rows, WIDTH), F32),
            pltpu.VMEM((rows, WIDTH), BF16),
            pltpu.VMEM((rows, WIDTH), BF16),
            pltpu.VMEM((rows, WIDTH), F32),
            pltpu.VMEM((rows, WIDTH), F32),
            pltpu.VMEM((rows, CHUNK), BF16),
            pltpu.VMEM((rows, CHUNK), BF16),
            pltpu.VMEM((rows, WIDTH), BF16),
            pltpu.VMEM((WIDTH, WIDTH), BF16),
            pltpu.VMEM((GROUPS, rows, COLS), BF16),
        ],
    )
    return pl.pallas_call(
        ffn_kernel,
        grid_spec=grid_spec,
        out_shape=(
            low(SEQS, BLOCK, WIDTH), full(SEQS, BLOCK, WIDTH),
            low(SEQS, BLOCK, COLS), low(SEQS, BLOCK + 128, COLS), low(SEQS, BLOCK + 128, COLS),
            low(2, FF // 2, WIDTH), low(2, FF // 2, WIDTH),
            low(WIDTH // 2, WIDTH), low(WIDTH // 2, WIDTH),
            full(8, WIDTH),
        ),
        compiler_params=params(60),
        cost_estimate=cost(2.4e10, 3e7),
        name="ffn",
    )(info, x, cotangent, *pieces, w_out, gain, bias, w_up, w_down)


def input_kernel(s, info, x, grad_middle, d0, d_next, d_over, d_prev, d_under, w_groups, gain, *rest):
    out = rest[-1]
    here = info[0]

    def w_of(ahead):
        return w_groups[lax.rem(here + ahead, GROUPS)]

    unit, inverse = unit_rows(x[0].astype(F32))
    over = jnp.concatenate([d_over[...], d_under[...]], axis=0)
    grad_normed = dot(d0[...], w_of(0), NN)
    grad_normed += dot(d_next[0:BLOCK, :], w_of(3), NN)
    grad_normed += dot(d_prev[0:BLOCK, :], w_of(1), NN)
    grad_normed += dot(over, w_of(2), NN)
    scaled = grad_normed * gain[...]
    mean_grad = jnp.mean(scaled, axis=-1, keepdims=True)
    mean_dot = jnp.mean(scaled * unit, axis=-1, keepdims=True)
    out[0] = grad_middle[0] + inverse * (scaled - mean_grad - unit * mean_dot)


def input_grad_of(s, info, x, grad_middle, pieces, w_groups, gain, earlier):
    one = lambda: pl.BlockSpec((1, BLOCK, WIDTH), lambda i, sc: (s, 0, 0))
    whole = lambda shape: pl.BlockSpec(shape, lambda i, sc: (0,) * len(shape))
    extra = [] if earlier is None else [earlier]
    return pl.pallas_call(
        functools.partial(input_kernel, s),
        grid_spec=pltpu.PrefetchScalarGridSpec(
            num_scalar_prefetch=1,
            grid=(1,),
            in_specs=[one(), one()]
            + [whole(p.shape) for p in pieces]
            + [whole(w_groups.shape), whole((1, WIDTH))]
            + [pl.BlockSpec(memory_space=pl.ANY)] * len(extra),
            out_specs=one(),
        ),
        out_shape=jax.ShapeDtypeStruct((SEQS, BLOCK, WIDTH), F32),
        input_output_aliases={} if earlier is None else {10: 0},
        compiler_params=params(40),
        cost_estimate=cost(1e9, 6e6),
        name="input_grad",
    )(info, x, grad_middle, *pieces, w_groups, gain, *extra)


def place_kernel(info, up_a, down_a, out_a, up_b, down_b, out_b, grad_up, grad_down, grad_out):
    mine = (pl.program_id(0) // 3) == info[1]

    @pl.when(mine)
    def _():
        grad_up[...] = jnp.transpose(up_a[...].astype(F32))
        grad_down[...] = down_a[...].astype(F32)
        grad_out[...] = out_a[...].astype(F32)

    @pl.when(jnp.logical_not(mine))
    def _():
        grad_up[...] = jnp.transpose(up_b[...].astype(F32))
        grad_down[...] = down_b[...].astype(F32)
        grad_out[...] = out_b[...].astype(F32)


def place(info, own, other):
    half = FF // CHUNK // 2

    def spec(rows, base, is_own):
        def index(i, sc):
            mine = (i // half) == sc[1] if is_own else (i // half) != sc[1]
            first = jnp.where(i < half, 0, half - 1)
            return (base + jnp.where(mine, lax.rem(i, half), first), 0)

        return pl.BlockSpec((rows, WIDTH), index)

    def three(is_own):
        return [spec(CHUNK, 0, is_own), spec(CHUNK, half, is_own), spec(128, 24, is_own)]

    return pl.pallas_call(
        place_kernel,
        grid_spec=pltpu.PrefetchScalarGridSpec(
            num_scalar_prefetch=1,
            grid=(2 * half,),
            in_specs=three(True) + three(False),
            out_specs=[
                pl.BlockSpec((WIDTH, CHUNK), lambda i, sc: (0, i)),
                pl.BlockSpec((CHUNK, WIDTH), lambda i, sc: (i, 0)),
                pl.BlockSpec((128, WIDTH), lambda i, sc: (i, 0)),
            ],
        ),
        out_shape=(
            jax.ShapeDtypeStruct((WIDTH, FF), F32),
            jax.ShapeDtypeStruct((FF, WIDTH), F32),
            jax.ShapeDtypeStruct((WIDTH, WIDTH), F32),
        ),
        compiler_params=params(40),
        cost_estimate=cost(1e6, 3.2e7),
        name="place",
    )(info, own, own, own, other, other, other)


def shift(array, axis, by):
    return lax.ppermute(array, axis, [(i, (i + by) % GROUPS) for i in range(GROUPS)])


def gather_rows(rows):
    ahead = shift(rows, "head", -1)
    behind = shift(rows, "head", 1)
    over_lo = shift(ahead[:128], "head", -1)
    over_hi = shift(behind[128:], "head", 1)
    return rows, ahead, over_lo, over_hi, behind


def exchange(own, to_next, to_prev):
    from_prev = shift(to_next, "head", 1)
    from_next = shift(to_prev, "head", -1)
    over = shift(from_prev[BLOCK:], "head", 1)
    under = shift(from_next[BLOCK:], "head", -1)
    return own, from_prev, over, from_next, under


def swap_cores(array):
    return lax.ppermute(array, "core", [(0, 1), (1, 0)])


def add_low(*terms):
    total = terms[0].astype(F32)
    for term in terms[1:]:
        total = total + term.astype(F32)
    return total.astype(BF16)


def scatter_sum(array, axis):
    me = lax.axis_index(axis)
    quarters = array.reshape(GROUPS, array.shape[0] // GROUPS, *array.shape[1:])
    pick = lambda k: lax.dynamic_index_in_dim(quarters, lax.rem(me + k, GROUPS), 0, False)
    return add_low(pick(0), *(shift(pick(k), axis, k) for k in (1, 2, 3)))


def gather_all(array, axis):
    me = lax.axis_index(axis)
    parts = [array] + [shift(array, axis, -k) for k in (1, 2, 3)]
    out = jnp.zeros((GROUPS, *array.shape), array.dtype)
    for k, part in enumerate(parts):
        out = lax.dynamic_update_index_in_dim(out, part, lax.rem(me + k, GROUPS), 0)
    return out.reshape(GROUPS * array.shape[0], *array.shape[1:])


def per_device(
    layer_input, lengths, cotangent, w_query, w_key, w_value, conv_query, conv_key, conv_value,
    w_out, w_up, w_down, gain_attn, bias_attn, gain_ffn, bias_ffn,
):
    here = lax.axis_index("head").astype(jnp.int32)
    core = lax.axis_index("core").astype(jnp.int32)
    gathered = [gather_rows(layer_input[s]) for s in range(SEQS)]

    w_groups = jnp.concatenate(
        [w.T.reshape(GROUPS, COLS, WIDTH) for w in (w_query, w_key, w_value)], axis=1
    )
    w_mine = lax.dynamic_index_in_dim(w_groups, here, 0, False)
    taps = lax.dynamic_slice_in_dim(
        jnp.concatenate([conv_query, conv_key, conv_value], axis=0), here * COLS, COLS, 1
    )
    gain_a, bias_a, gain_f, bias_f = (
        v.reshape(1, WIDTH) for v in (gain_attn, bias_attn, gain_ffn, bias_ffn)
    )
    infos = [jnp.stack([here, lengths[s]]) for s in range(SEQS)]
    info_all = jnp.concatenate([jnp.stack([here, core]), lengths])

    saved, pieces = [], []
    for s in range(SEQS):
        normed, raw_q, raw_k, raw_v, mixed, m0, m_next, m_prev, lse_t = attend(
            infos[s], gathered[s], w_mine, taps, gain_a, bias_a
        )
        saved.append((normed, raw_q, raw_k, raw_v, mixed, lse_t))
        pieces.extend(exchange(m0, m_next, m_prev))

    (
        layer_output, grad_middle, g0, g_next, g_prev, send, keep, send_out, keep_out, vectors,
    ) = ffn(info_all, layer_input, cotangent, pieces, w_out, gain_f, bias_f, w_up, w_down)

    half_sum = jnp.concatenate(
        [
            add_low(keep, swap_cores(send)).reshape(FF, WIDTH),
            add_low(keep_out, swap_cores(send_out)),
        ],
        axis=0,
    )
    half_sum = lax.psum(half_sum, ("x", "z", "head"))
    grad_up, grad_down, grad_out = place(info_all, half_sum, swap_cores(half_sum))

    dw = jnp.zeros((3 * COLS, WIDTH), F32)
    small = jnp.zeros((16, WIDTH), F32)
    input_grad = None
    for s in range(SEQS):
        grads = exchange(g0[s], g_next[s], g_prev[s])
        results = attend_back(
            s == 0, s == SEQS - 1, infos[s], grads, saved[s], w_mine, taps, gain_a, bias_a, vectors, dw, small
        )
        d0, d_next, d_prev, dw, small = results[:5]
        input_grad = input_grad_of(
            s, info_all, layer_input, grad_middle, exchange(d0, d_next, d_prev), w_groups, gain_a, input_grad
        )
    pack = results[5]

    half = PACK_ROWS // 2
    part = add_low(
        lax.dynamic_slice_in_dim(pack, core * half, half, 0),
        swap_cores(lax.dynamic_slice_in_dim(pack, (1 - core) * half, half, 0)),
    )
    part = scatter_sum(scatter_sum(part, "x"), "z")
    part = gather_all(gather_all(part, "z"), "x")
    part = gather_all(part[None], "head")
    other = swap_cores(part)
    pair = jnp.stack([part, other], axis=1)
    pair = jnp.where(core == 0, pair, pair[:, ::-1])
    whole = pair.reshape(GROUPS, PACK_ROWS, WIDTH).astype(F32)

    def weight(n):
        return whole[:, n * COLS : (n + 1) * COLS, :].reshape(WIDTH, WIDTH).T

    def conv(n):
        rows = whole[:, 3 * COLS + 3 * n : 3 * COLS + 3 * n + 3, 0:COLS]
        return jnp.transpose(rows, (1, 0, 2)).reshape(3, WIDTH)

    vector = jnp.sum(whole[:, 3 * COLS + 9 : 3 * COLS + 13, :], axis=0)
    return (
        layer_output,
        input_grad,
        weight(0), weight(1), weight(2),
        conv(0), conv(1), conv(2),
        grad_out, grad_up, grad_down,
        vector[0], vector[1], vector[2], vector[3],
    )


def solution(mesh):
    fine = Mesh(mesh.devices.reshape(4, 4, 2, GROUPS), ("x", "z", "core", "head"))
    dp = ("x", "z", "core")
    rows = P(dp, "head", None)
    return jax.shard_map(
        per_device,
        mesh=fine,
        in_specs=(rows, P(dp), rows) + (P(),) * 13,
        out_specs=(rows, rows) + (P(),) * 13,
        check_vma=False,
    )
```

time: 903 us -> 496 us (0.55)
  matrix products: 179 us -> 0 us
  waiting for transfers between devices: 241 us -> 112 us
  Pallas kernels: 0 us -> 120 us
  other arithmetic: 133 us -> 23.4 us
  local copies, waits for them, and re-layouts: 206 us -> 111 us
  starting transfers between devices: 34.5 us -> 106 us
  blocking collectives: 68.9 us -> 0 us
  loops' own time: 19.5 us -> 0 us
    dot_general x60 -> x0, matrix products: 179 us -> none  [the longest x6 35.5 us: product_left_t(): lax.dot_general(left, right, (((0,), (0,)), ((), ())), preferred_element_...]
    psum x1, waiting for transfers between devices: 144 us -> 12.1 us  [per_device(): half_sum = lax.psum(half_sum, ('x', 'z', 'head'))]
    pallas_call x0 -> x11, Pallas kernels: none -> 120 us  [the longest x1 41.3 us: ffn(): pl.pallas_call(ffn_kernel, grid_spec=grid_spec, out_shape=(low(SEQS, BLOC...]
    ppermute x0 -> x68, starting transfers between devices: none -> 106 us  [the longest x63 105 us: shift(): lax.ppermute(array, axis, [(i, (i + by) % GROUPS) for i in range(GROUPS)])]
    ppermute x0 -> x68, waiting for transfers between devices: none -> 100 us  [the longest x63 89.8 us: shift(): lax.ppermute(array, axis, [(i, (i + by) % GROUPS) for i in range(GROUPS)])]
    all_to_all x8 -> x0, waiting for transfers between devices: 96.4 us -> none  [the longest x3 39.6 us: grouped_exchange(): lax.all_to_all(group, axis, split_axis=split_dim, concat_axis=concat_dim,...]
    psum x1 -> x0, blocking collectives: 68.9 us -> none  [per_device(): lax.psum((grad_w_query, grad_w_key, grad_w_value, grad_conv_query, grad_c...]
    reduce_sum x30 -> x1, other arithmetic: 46.5 us -> 0.92 us  [per_device(): vector = jnp.sum(whole[:, 3 * COLS + 9:3 * COLS + 13, :], axis=0)]
  transfers between devices with their start and end apart: 9 -> 69, of which waited for: 8 -> 21; matrix products, arithmetic and copies ran while one was open for 11% -> 18% of each run, Pallas kernels for 0% -> 14%
where the time goes in v1:
time: 496 us; the launch traced here: 488 us
  Pallas kernels  120 us (24%)
  waiting for transfers between devices  112 us (23%)
  local copies, waits for them, and re-layouts  111 us (22%)
  starting transfers between devices  106 us (21%)
  other arithmetic  23.4 us (5%)
  between operations  15.1 us (3%)
    ppermute x63, starting transfers between devices, shift(): lax.ppermute(array, axis, [(i, (i + by) % GROUPS) for i in range(GROUPS)])  105 us
    ppermute x63, waiting for transfers between devices, shift(): lax.ppermute(array, axis, [(i, (i + by) % GROUPS) for i in range(GROUPS)])  89.8 us
    unnamed x183, local copies, waits for them, and re-layouts  45.6 us
    pallas_call x1, Pallas kernels, ffn(): pl.pallas_call(ffn_kernel, grid_spec=grid_spec, out_shape=(low(SEQS, BLOC...  41.3 us
    pallas_call x3, Pallas kernels, attend_back(): pl.pallas_call(functools.partial(attend_back_kernel, first, last), out_sh...  37.9 us
    pallas_call x3, Pallas kernels, attend(): pl.pallas_call(attend_kernel, out_shape=(low(FULL, WIDTH), low(FULL, COLS...  17.3 us
    dynamic_update_slice x11, local copies, waits for them, and re-layouts, gather_all(): out = lax.dynamic_update_index_in_dim(out, part, lax.rem(me + k, GROUPS), 0)  13.7 us
    pallas_call x3, Pallas kernels, input_grad_of(): pl.pallas_call(functools.partial(input_kernel, s), grid_spec=pltpu.Prefet...  12.2 us
  transfers between devices with their start and end apart: 69, of which 21 were waited for; matrix products, arithmetic and copies ran while one was open for 18% of the time, Pallas kernels for 14%

profile of v1, /device:TPU:0, one launch (start us, length us, event | category | flops | bytes accessed | tf_op | source)
XLA Modules:
  0.0 487.5 jit_solution(7623613228437489272)
XLA Ops:
  23.9 7.7 %collective-permute-done.2.x3 = bf16[256,768]{1,0:T(8,128)(2,1)} collective-permute-done((bf16[256,768]{1,0:T(8,128)(2,1)}, bf16[256,768]{1,0:T(8,128)(2,1)}, u32[]{:S(2)}, u32[]{:S(2)}) %collective-permute-start.2) | collective-permute-done | bytes 393248 | tf_op jit(solution)/shard_map/ppermute | solution.py:583
  63.5 3.8 attend.4
  76.3 10.3 %attend.5 = (bf16[1024,768]{1,0:T(8,128)(2,1)S(1)}, bf16[1024,192]{1,0:T(8,128)(2,1)S(1)}, bf16[1024,192]{1,0:T(8,128)(2,1)S(1)}, bf16[1024,192]{1,0:T(8,128)(2,...) custom-call(s32[2]{0:T(128)S(1)} %pad_add_fusion.3.info, ...), custom_call_target="tpu_custom_call" | custom-call | flops 3000000000 | bytes 8000000 | tf_op jit(solution)/shard_map/attend/pallas_call | solution.py:152
  115.1 41.3 %ffn.1 = (bf16[3,256,768]{2,1,0:T(8,128)(2,1)}, f32[3,256,768]{2,1,0:T(8,128)}, bf16[3,256,192]{2,1,0:T(8,128)(2,1)}, bf16[3,384,192]{2,1,0:T(8,128)(2,1)}, bf16...) custom-call(s32[5]{0:T(128)} %pad_add_fusion.info, ...), custom_call_target="tpu_custom_call" | custom-call | flops 24000000000 | bytes 30000000 | tf_op jit(solution)/shard_map/ffn/pallas_call | solution.py:471
  157.1 8.3 %collective-permute-done.66 = bf16[384,768]{1,0:T(8,128)(2,1)S(1)} collective-permute-done((bf16[384,768]{1,0:T(8,128)(2,1)}, bf16[384,768]{1,0:T(8,128)(2,1)S(1)}, u32[]{:S(2)}, u32[]{:S(2)}) %collective-permute-start.66) | collective-permute-done | bytes 589856 | tf_op jit(solution)/shard_map/ppermute | solution.py:603
  192.3 5.3 %collective-permute-done.24.g_next = bf16[384,192]{1,0:T(8,128)(2,1)S(1)} collective-permute-done((bf16[384,192]{1,0:T(8,128)(2,1)}, bf16[384,192]{1,0:T(8,128)(2,1)S(1)}, u32[]{:S(2)}, u32[]{:S(2)}) %collective-permute-start.24) | collective-permute-done | bytes 147488 | tf_op jit(solution)/shard_map/ppermute | solution.py:583
  197.7 4.4 collective-permute-done.26.g_prev
  207.2 7.0 %attend_back.3 = (bf16[256,576]{1,0:T(8,128)(2,1)S(1)}, bf16[384,576]{1,0:T(8,128)(2,1)S(1)}, bf16[384,576]{1,0:T(8,128)(2,1)S(1)}, f32[576,768]{1,0:T(8,128)}, f32[16,768]{1,0:T(8,128)S(1)}) custom-call(s32[2]{0:T(128)S(1)} %pad_add_fusion.1.info, bf16[256,192]{1,0:T(8,128)(2,1)S(1)} %get-tuple-element.177.g0, ...), custom_call_target="tpu_custom_call" | custom-call | flops 5000000000 | bytes 12000000 | tf_op jit(solution)/shard_map/attend_back/pallas_call | solution.py:313
  216.6 12.7 %attend_back.4 = (bf16[256,576]{1,0:T(8,128)(2,1)S(1)}, bf16[384,576]{1,0:T(8,128)(2,1)S(1)}, bf16[384,576]{1,0:T(8,128)(2,1)S(1)}, f32[576,768]{1,0:T(8,128)}, f32[16,768]{1,0:T(8,128)S(1)}) custom-call(s32[2]{0:T(128)S(1)} %copy-done.38, bf16[256,192]{1,0:T(8,128)(2,1)S(1)} %get-tuple-element.178.g0, bf16[384,192]{1,0:T(8,128)(2,1)} %collective-permute-done.28.g_next, ...), custom_call_target="tpu_custom_call" | custom-call | flops 5000000000 | bytes 12000000 | tf_op jit(solution)/shard_map/attend_back/pallas_call | solution.py:313
  231.6 18.2 %attend_back.5 = (bf16[256,576]{1,0:T(8,128)(2,1)S(1)}, bf16[384,576]{1,0:T(8,128)(2,1)S(1)}, bf16[384,576]{1,0:T(8,128)(2,1)S(1)}, f32[576,768]{1,0:T(8,128)}, ...) custom-call(s32[2]{0:T(128)S(1)} %pad_add_fusion.3.info, bf16[256,192]{1,0:T(8,128)(2,1)S(1)} %get-tuple-element.179.g0, ...), custom_call_target="tpu_custom_call" | custom-call | flops 5000000000 | bytes 12000000 | tf_op jit(solution)/shard_map/attend_back/pallas_call | solution.py:313
  257.5 5.3 %collective-permute-start.49 = (bf16[80,768]{1,0:T(8,128)(2,1)}, bf16[80,768]{1,0:T(8,128)(2,1)}, u32[]{:S(2)}, u32[]{:S(2)}) collective-permute-start(bf16[80,768]{1,0:T(8,128)(2,1)} %get-tuple-element.174), channel_id=1, source_target_pairs={{0,32},{32,64},{64,96},{96,0},{1,33},{33,65},{65,97},{97,1},{2,34}... | collective-permute-start | bytes 368648 | tf_op jit(solution)/shard_map/ppermute | solution.py:583
  274.5 10.3 %collective-permute-start.52 = (bf16[20,768]{1,0:T(8,128)(2,1)}, bf16[20,768]{1,0:T(8,128)(2,1)}, u32[]{:S(2)}, u32[]{:S(2)}) collective-permute-start(bf16[20,768]{1,0:T(8,128)(2,1)} %get-tuple-element.180), channel_id=1, source_target_pairs={{0,8},{8,16},{16,24},{24,0},{1,9},{9,17},{17,25},{25,1},{2,10},{10... | collective-permute-start | bytes 92168 | tf_op jit(solution)/shard_map/ppermute | solution.py:583
  284.8 7.1 %collective-permute-start.54 = (bf16[20,768]{1,0:T(8,128)(2,1)}, bf16[20,768]{1,0:T(8,128)(2,1)}, u32[]{:S(2)}, u32[]{:S(2)}) collective-permute-start(bf16[20,768]{1,0:T(8,128)(2,1)} %get-tuple-element.181), channel_id=1, source_target_pairs={{0,24},{8,0},{16,8},{24,16},{1,25},{9,1},{17,9},{25,17},{2,26},{10... | collective-permute-start | bytes 92168 | tf_op jit(solution)/shard_map/ppermute | solution.py:583
  323.8 12.1 %all-reduce.2.cloned.1.call-done.up_a.down_a.out_a = bf16[3456,768]{1,0:T(8,128)(2,1)} async-done(((bf16[3456,768]{1,0:T(8,128)(2,1)}), bf16[3456,768]{1,0:T(8,128)(2,1)}) %all-reduce.2.cloned.1.call-update) | async-done | bytes 5308432 | tf_op jit(solution)/shard_map/psum | solution.py:669
  343.9 17.6 %collective-permute-done.61 = bf16[1,320,768]{2,1,0:T(8,128)(2,1)} collective-permute-done((bf16[1,320,768]{2,1,0:T(8,128)(2,1)}, bf16[1,320,768]{2,1,0:T(8,128)(2,1)}, u32[]{:S(2)}, u32[]{:S(2)}) %collective-permute-start.61) | collective-permute-done | bytes 491552 | tf_op jit(solution)/shard_map/ppermute | solution.py:583
  366.7 4.4 collective-permute-start.44
  371.1 10.7 %collective-permute-done.36.d_next = bf16[384,576]{1,0:T(8,128)(2,1)} collective-permute-done((bf16[384,576]{1,0:T(8,128)(2,1)S(1)}, bf16[384,576]{1,0:T(8,128)(2,1)}, u32[]{:S(2)}, u32[]{:S(2)}) %collective-permute-start.36) | collective-permute-done | bytes 442400 | tf_op jit(solution)/shard_map/ppermute | solution.py:583
  383.8 8.5 %collective-permute-done.40.d_next = bf16[384,576]{1,0:T(8,128)(2,1)S(1)} collective-permute-done((bf16[384,576]{1,0:T(8,128)(2,1)S(1)}, bf16[384,576]{1,0:T(8,128)(2,1)S(1)}, u32[]{:S(2)}, u32[]{:S(2)}) %collective-permute-start.40) | collective-permute-done | bytes 442400 | tf_op jit(solution)/shard_map/ppermute | solution.py:583
  394.3 8.4 %collective-permute-done.44.d_next = bf16[384,576]{1,0:T(8,128)(2,1)S(1)} collective-permute-done((bf16[384,576]{1,0:T(8,128)(2,1)S(1)}, bf16[384,576]{1,0:T(8,128)(2,1)S(1)}, u32[]{:S(2)}, u32[]{:S(2)}) %collective-permute-start.44) | collective-permute-done | bytes 442400 | tf_op jit(solution)/shard_map/ppermute | solution.py:583
  408.4 7.4 %collective-permute-done.42.d_prev = bf16[384,576]{1,0:T(8,128)(2,1)S(1)} collective-permute-done((bf16[384,576]{1,0:T(8,128)(2,1)S(1)}, bf16[384,576]{1,0:T(8,128)(2,1)S(1)}, u32[]{:S(2)}, u32[]{:S(2)}) %collective-permute-start.42) | collective-permute-done | bytes 442400 | tf_op jit(solution)/shard_map/ppermute | solution.py:583
  433.1 4.0 input_grad.3.rest_0_
  437.1 4.0 input_grad.4.rest_0_
  441.1 4.2 input_grad.5
  469.3 11.2 %place.1 = (f32[768,3072]{1,0:T(8,128)}, f32[3072,768]{1,0:T(8,128)}, f32[768,768]{1,0:T(8,128)}) custom-call(s32[5]{0:T(128)S(1)} %copy-done.24, bf16[3456,768]{1,0:T(8,128)(2,1)S(1)} %copy-done, bf16[3456,768]{1,0:T(8,128)(2,1)S(1)} %copy-done, bf16[3456,768]{1,0:T(8,128)(2,1)S(1)} %copy-done, bf16[3456,768]{1,0:T(8,128)(2,1)} %collective-permute-done.67.up_b.down_b.out_b, ...), custom_call_target="tpu_custom_call" | custom-call | flops 1000000 | bytes 32000000 | tf_op jit(solution)/shard_map/place/pallas_call | solution.py:559
  (393 shorter events, 238.3 us)
Async XLA Ops:
  7.2 328.7 %all-reduce.2.cloned.1.call-start = ((), (), s32[]{:S(2)}) async-start(), calls=%async_computation | async-start | bytes 10616832 | tf_op jit(solution)/shard_map/psum | solution.py:669
  9.7 28.2 %collective-permute-start.18 = (bf16[256,768]{1,0:T(8,128)(2,1)}, bf16[256,768]{1,0:T(8,128)(2,1)}, u32[]{:S(2)}, u32[]{:S(2)}) collective-permute-start(bf16[256,768]{1,0:T(8,128)(2,1)} %get-tuple-element.165.x0), channel_id=1, source_target_pairs={{0,1},{1,2},{2,3},{3,0},{4,5},{5,6},{6,7},{7,4},{8,9},{9,10},{10,1... | collective-permute-start | bytes 1179656 | tf_op jit(solution)/shard_map/ppermute | solution.py:583
  11.3 31.7 %collective-permute-start.16 = (bf16[256,768]{1,0:T(8,128)(2,1)}, bf16[256,768]{1,0:T(8,128)(2,1)}, u32[]{:S(2)}, u32[]{:S(2)}) collective-permute-start(bf16[256,768]{1,0:T(8,128)(2,1)} %get-tuple-element.165.x0), channel_id=1, source_target_pairs={{0,3},{1,0},{2,1},{3,2},{4,7},{5,4},{6,5},{7,6},{8,11},{9,8},{10,9... | collective-permute-start | bytes 1179656 | tf_op jit(solution)/shard_map/ppermute | solution.py:583
  13.3 23.3 %collective-permute-start = (bf16[256,768]{1,0:T(8,128)(2,1)}, bf16[256,768]{1,0:T(8,128)(2,1)}, u32[]{:S(2)}, u32[]{:S(2)}) collective-permute-start(bf16[256,768]{1,0:T(8,128)(2,1)} %get-tuple-element.167.x0), channel_id=1, source_target_pairs={{0,3},{1,0},{2,1},{3,2},{4,7},{5,4},{6,5},{7,6},{8,11},{9,8},{10,9... | collective-permute-start | bytes 1179656 | tf_op jit(solution)/shard_map/ppermute | solution.py:583
  16.1 27.9 %collective-permute-start.10 = (bf16[256,768]{1,0:T(8,128)(2,1)}, bf16[256,768]{1,0:T(8,128)(2,1)}, u32[]{:S(2)}, u32[]{:S(2)}) collective-permute-start(bf16[256,768]{1,0:T(8,128)(2,1)} %get-tuple-element.166.x0), channel_id=1, source_target_pairs={{0,1},{1,2},{2,3},{3,0},{4,5},{5,6},{6,7},{7,4},{8,9},{9,10},{10,1... | collective-permute-start | bytes 1179656 | tf_op jit(solution)/shard_map/ppermute | solution.py:583
  43.0 29.9 %collective-permute-start.19 = (bf16[128,768]{1,0:T(8,128)(2,1)S(1)}, bf16[128,768]{1,0:T(8,128)(2,1)S(1)}, u32[]{:S(2)}, u32[]{:S(2)}) collective-permute-start(bf16[128,768]{1,0:T(8,128)(2,1)S(1)} %slice.209), channel_id=1, source_target_pairs={{0,1},{1,2},{2,3},{3,0},{4,5},{5,6},{6,7},{7,4},{8,9},{9,10},{10,1... | collective-permute-start | bytes 589832 | tf_op jit(solution)/shard_map/ppermute | solution.py:583
  44.0 32.3 %collective-permute-start.17 = (bf16[128,768]{1,0:T(8,128)(2,1)S(1)}, bf16[128,768]{1,0:T(8,128)(2,1)S(1)}, u32[]{:S(2)}, u32[]{:S(2)}) collective-permute-start(bf16[128,768]{1,0:T(8,128)(2,1)S(1)} %slice.208), channel_id=1, source_target_pairs={{0,3},{1,0},{2,1},{3,2},{4,7},{5,4},{6,5},{7,6},{8,11},{9,8},{10,9... | collective-permute-start | bytes 589832 | tf_op jit(solution)/shard_map/ppermute | solution.py:583
  60.3 31.4 %collective-permute-start.4 = (bf16[384,192]{1,0:T(8,128)(2,1)S(1)}, bf16[384,192]{1,0:T(8,128)(2,1)S(1)}, u32[]{:S(2)}, u32[]{:S(2)}) collective-permute-start(bf16[384,192]{1,0:T(8,128)(2,1)S(1)} %get-tuple-element.70), channel_id=1, source_target_pairs={{0,1},{1,2},{2,3},{3,0},{4,5},{5,6},{6,7},{7,4},{8,9},{9,10},{10,1... | collective-permute-start | bytes 442376 | tf_op jit(solution)/shard_map/ppermute | solution.py:583
  60.3 35.3 %collective-permute-start.6 = (bf16[384,192]{1,0:T(8,128)(2,1)S(1)}, bf16[384,192]{1,0:T(8,128)(2,1)S(1)}, u32[]{:S(2)}, u32[]{:S(2)}) collective-permute-start(bf16[384,192]{1,0:T(8,128)(2,1)S(1)} %get-tuple-element.71), channel_id=1, source_target_pairs={{0,3},{1,0},{2,1},{3,2},{4,7},{5,4},{6,5},{7,6},{8,11},{9,8},{10,9... | collective-permute-start | bytes 442376 | tf_op jit(solution)/shard_map/ppermute | solution.py:583
  72.9 24.2 %collective-permute-start.12 = (bf16[384,192]{1,0:T(8,128)(2,1)}, bf16[384,192]{1,0:T(8,128)(2,1)}, u32[]{:S(2)}, u32[]{:S(2)}) collective-permute-start(bf16[384,192]{1,0:T(8,128)(2,1)} %get-tuple-element.73), channel_id=1, source_target_pairs={{0,1},{1,2},{2,3},{3,0},{4,5},{5,6},{6,7},{7,4},{8,9},{9,10},{10,1... | collective-permute-start | bytes 442376 | tf_op jit(solution)/shard_map/ppermute | solution.py:583
  72.9 28.3 %collective-permute-start.14 = (bf16[384,192]{1,0:T(8,128)(2,1)}, bf16[384,192]{1,0:T(8,128)(2,1)}, u32[]{:S(2)}, u32[]{:S(2)}) collective-permute-start(bf16[384,192]{1,0:T(8,128)(2,1)} %get-tuple-element.74), channel_id=1, source_target_pairs={{0,3},{1,0},{2,1},{3,2},{4,7},{5,4},{6,5},{7,6},{8,11},{9,8},{10,9... | collective-permute-start | bytes 442376 | tf_op jit(solution)/shard_map/ppermute | solution.py:583
  186.3 19.4 %collective-permute-start.33 = (bf16[128,192]{1,0:T(8,128)(2,1)S(1)}, bf16[128,192]{1,0:T(8,128)(2,1)S(1)}, u32[]{:S(2)}, u32[]{:S(2)}) collective-permute-start(bf16[128,192]{1,0:T(8,128)(2,1)S(1)} %slice.216), channel_id=1, source_target_pairs={{0,1},{1,2},{2,3},{3,0},{4,5},{5,6},{6,7},{7,4},{8,9},{9,10},{10,1... | collective-permute-start | bytes 147464 | tf_op jit(solution)/shard_map/ppermute | solution.py:583
  197.7 33.9 %collective-permute-start.25 = (bf16[128,192]{1,0:T(8,128)(2,1)S(1)}, bf16[128,192]{1,0:T(8,128)(2,1)S(1)}, u32[]{:S(2)}, u32[]{:S(2)}) collective-permute-start(bf16[128,192]{1,0:T(8,128)(2,1)S(1)} %slice.212), channel_id=1, source_target_pairs={{0,1},{1,2},{2,3},{3,0},{4,5},{5,6},{6,7},{7,4},{8,9},{9,10},{10,1... | collective-permute-start | bytes 147464 | tf_op jit(solution)/shard_map/ppermute | solution.py:583
  205.7 25.9 %collective-permute-start.27 = (bf16[128,192]{1,0:T(8,128)(2,1)S(1)}, bf16[128,192]{1,0:T(8,128)(2,1)S(1)}, u32[]{:S(2)}, u32[]{:S(2)}) collective-permute-start(bf16[128,192]{1,0:T(8,128)(2,1)S(1)} %slice.213), channel_id=1, source_target_pairs={{0,3},{1,0},{2,1},{3,2},{4,7},{5,4},{6,5},{7,6},{8,11},{9,8},{10,9... | collective-permute-start | bytes 147464 | tf_op jit(solution)/shard_map/ppermute | solution.py:583
  274.5 19.6 %collective-permute-start.52 = (bf16[20,768]{1,0:T(8,128)(2,1)}, bf16[20,768]{1,0:T(8,128)(2,1)}, u32[]{:S(2)}, u32[]{:S(2)}) collective-permute-start(bf16[20,768]{1,0:T(8,128)(2,1)} %get-tuple-element.180), channel_id=1, source_target_pairs={{0,8},{8,16},{16,24},{24,0},{1,9},{9,17},{17,25},{25,1},{2,10},{10... | collective-permute-start | bytes 92168 | tf_op jit(solution)/shard_map/ppermute | solution.py:583
  313.9 22.0 %collective-permute-start.60 = (bf16[80,768]{1,0:T(8,128)(2,1)}, bf16[80,768]{1,0:T(8,128)(2,1)}, u32[]{:S(2)}, u32[]{:S(2)}) collective-permute-start(bf16[80,768]{1,0:T(8,128)(2,1)} %reshape.102), channel_id=1, source_target_pairs={{0,32},{32,64},{64,96},{96,0},{1,33},{33,65},{65,97},{97,1},{2,34}... | collective-permute-start | bytes 368648 | tf_op jit(solution)/shard_map/ppermute | solution.py:583
  335.9 130.9 %collective-permute-start.67 = (bf16[3456,768]{1,0:T(8,128)(2,1)}, bf16[3456,768]{1,0:T(8,128)(2,1)}, u32[]{:S(2)}, u32[]{:S(2)}) collective-permute-start(bf16[3456,768]{1,0:T(8,128)(2,1)} %all-reduce.2.cloned.1.call-done.up_a.down_a.out_a), channel_id=1, source_target_pairs={{0,4},{4,0},{1,5},{5,1},{2,6},{6,2},{3,7},{7,3},{8,12},{12,8},{9,1... | collective-permute-start | bytes 15925256 | tf_op jit(solution)/shard_map/ppermute | solution.py:603
  337.5 24.1 %collective-permute-start.61 = (bf16[1,320,768]{2,1,0:T(8,128)(2,1)}, bf16[1,320,768]{2,1,0:T(8,128)(2,1)}, u32[]{:S(2)}, u32[]{:S(2)}) collective-permute-start(bf16[1,320,768]{2,1,0:T(8,128)(2,1)} %bitcast.38), channel_id=1, source_target_pairs={{0,3},{1,0},{2,1},{3,2},{4,7},{5,4},{6,5},{7,6},{8,11},{9,8},{10,9... | collective-permute-start | bytes 1474568 | tf_op jit(solution)/shard_map/ppermute | solution.py:583
  339.5 23.9 %collective-permute-start.62 = (bf16[1,320,768]{2,1,0:T(8,128)(2,1)}, bf16[1,320,768]{2,1,0:T(8,128)(2,1)}, u32[]{:S(2)}, u32[]{:S(2)}) collective-permute-start(bf16[1,320,768]{2,1,0:T(8,128)(2,1)} %bitcast.38), channel_id=1, source_target_pairs={{0,2},{1,3},{2,0},{3,1},{4,6},{5,7},{6,4},{7,5},{8,10},{9,11},{10,... | collective-permute-start | bytes 1474568 | tf_op jit(solution)/shard_map/ppermute | solution.py:583
  340.3 24.9 %collective-permute-start.63 = (bf16[1,320,768]{2,1,0:T(8,128)(2,1)}, bf16[1,320,768]{2,1,0:T(8,128)(2,1)S(1)}, u32[]{:S(2)}, u32[]{:S(2)}) collective-permute-start(bf16[1,320,768]{2,1,0:T(8,128)(2,1)} %bitcast.38), channel_id=1, source_target_pairs={{0,1},{1,2},{2,3},{3,0},{4,5},{5,6},{6,7},{7,4},{8,9},{9,10},{10,1... | collective-permute-start | bytes 1474568 | tf_op jit(solution)/shard_map/ppermute | solution.py:583
  366.0 79.3 %collective-permute-start.64 = (bf16[4,320,768]{2,1,0:T(8,128)(2,1)}, bf16[4,320,768]{2,1,0:T(8,128)(2,1)}, u32[]{:S(2)}, u32[]{:S(2)}) collective-permute-start(bf16[4,320,768]{2,1,0:T(8,128)(2,1)} %bitcast.42), channel_id=1, source_target_pairs={{0,4},{4,0},{1,5},{5,1},{2,6},{6,2},{3,7},{7,3},{8,12},{12,8},{9,1... | collective-permute-start | bytes 5898248 | tf_op jit(solution)/shard_map/ppermute | solution.py:603
  366.1 26.2 %collective-permute-start.40 = (bf16[384,576]{1,0:T(8,128)(2,1)S(1)}, bf16[384,576]{1,0:T(8,128)(2,1)S(1)}, u32[]{:S(2)}, u32[]{:S(2)}) collective-permute-start(bf16[384,576]{1,0:T(8,128)(2,1)S(1)} %copy-done.32), channel_id=1, source_target_pairs={{0,1},{1,2},{2,3},{3,0},{4,5},{5,6},{6,7},{7,4},{8,9},{9,10},{10,1... | collective-permute-start | bytes 1327112 | tf_op jit(solution)/shard_map/ppermute | solution.py:583
  366.7 35.9 %collective-permute-start.44 = (bf16[384,576]{1,0:T(8,128)(2,1)S(1)}, bf16[384,576]{1,0:T(8,128)(2,1)S(1)}, u32[]{:S(2)}, u32[]{:S(2)}) collective-permute-start(bf16[384,576]{1,0:T(8,128)(2,1)S(1)} %copy-done.28), channel_id=1, source_target_pairs={{0,1},{1,2},{2,3},{3,0},{4,5},{5,6},{6,7},{7,4},{8,9},{9,10},{10,1... | collective-permute-start | bytes 1327112 | tf_op jit(solution)/shard_map/ppermute | solution.py:583
  381.9 23.3 %collective-permute-start.46 = (bf16[384,576]{1,0:T(8,128)(2,1)S(1)}, bf16[384,576]{1,0:T(8,128)(2,1)S(1)}, u32[]{:S(2)}, u32[]{:S(2)}) collective-permute-start(bf16[384,576]{1,0:T(8,128)(2,1)S(1)} %copy-done.26), channel_id=1, source_target_pairs={{0,3},{1,0},{2,1},{3,2},{4,7},{5,4},{6,5},{7,6},{8,11},{9,8},{10,9... | collective-permute-start | bytes 1327112 | tf_op jit(solution)/shard_map/ppermute | solution.py:583
  (135 other events, 1418.7 us)
Sparse Core Ops, SparseCore 0:
  173.0 162.7 all-reduce.1
